TPU v7x, 32 devices: a whole 2x2x4 slice. The times are simulated.
32 devices in a mesh: req: 8 (over z, x), head: 4 (over y, core).
Axes of the slice: x: 2, y: 2, z: 4, core: 2. Of those that a mesh axis runs over, the one named last changes fastest.
Arguments:
- prompt_query_latents: bfloat16 [4096, 1536], P(('req', 'head')), may hold values from -6 to 6
- prompt_latents: bfloat16 [4096, 512], P(('req', 'head')), may hold values from -320 to 320
- prompt_rotary_keys: bfloat16 [64, 4096], P(None, ('req', 'head')), may hold values from -6 to 6
- positions: int32 [4096], P(('req', 'head')), may hold values from 0 to 511, as said below
- query_up_weight: bfloat16 [1536, 12288], P(None, 'head'), may hold values from -0.15625 to 0.15625
- key_up_weight: bfloat16 [512, 8192], P(None, 'head'), may hold values from -0.25 to 0.25
- value_up_weight: bfloat16 [512, 8192], P(None, 'head'), may hold values from -0.25 to 0.25
- decode_queries: bfloat16 [512, 12288], P('req', 'head'), may hold values from -6 to 6
- decode_owner_index: int32 [512], P('req'), may hold values from 0 to 7, as said below
- decode_cache_slot: int32 [512], P('req'), may hold values from 0 to 63, as said below
- latent_cache_rows: bfloat16 [512, 256, 512], P('req'), may hold values from -320 to 320
- rotated_cache_keys: bfloat16 [512, 64, 256], P('req'), may hold values from -6 to 6
- cache_live_lengths: int32 [512], P('req'), may hold values from 1 to 256
Outputs:
- prompt_attention_output: bfloat16 [4096, 8192], P('req', 'head')
- decode_out: bfloat16 [512, 8192], P('req', 'head')
Inputs may be any that keep to these rules, and one draw needn't show every extreme that they name: `positions`: a position is 0 where a prompt begins, always at the first token of a block and, from the second block on, at other tokens too, and otherwise one more than the previous token's; the first block holds one whole prompt. `decode_owner_index`: each entry device's 64 requests name 4 owners, each exactly 16 times; every pair of owner and slot is named by exactly one request. `decode_cache_slot`: see decode_owner_index.
All inputs are finite; a program needn't handle non-finite values.
Results may differ from a plain program's by a relative error of at most 0.012.
The roundings to bfloat16 on the way count: a program that leaves them out, or rounds other values in their place, can miss the bound.
Values may be sent and summed in bfloat16 or wider, within the bound.
A program may use at most 192 MiB of HBM per device.

v0:
```python
import jax
import jax.numpy as jnp
from jax import lax
from jax.sharding import PartitionSpec as P

D_C = 512
D_NOPE = 128
D_ROPE = 64
D_V = 128


ROPE_BASE = 10000.0


def rotate(values, position):
    half_width = values.shape[-1] // 2
    frequency = ROPE_BASE ** (-jnp.arange(half_width, dtype=jnp.float32) / half_width)
    angles = position.astype(jnp.float32)[..., None] * frequency
    cosines = jnp.cos(angles)
    sine_term = jnp.sin(angles)
    first_half = values[..., :half_width]
    second_half = values[..., half_width:]
    return jnp.concatenate(
        [
            first_half * cosines - second_half * sine_term,
            first_half * sine_term + second_half * cosines,
        ],
        axis=-1,
    )


def prompt_prefill(
    prompt_query_latents,
    prompt_latents,
    prompt_rotary_keys,
    positions,
    query_up_weight,
    key_up_weight,
    value_up_weight,
):
    score_scale = (D_NOPE + D_ROPE) ** (-0.5)
    rows_query, rows_latent, rows_rope, rows_place = (
        lax.all_gather(prompt_query_latents, "head", axis=0, tiled=True),
        lax.all_gather(prompt_latents, "head", axis=0, tiled=True),
        lax.all_gather(prompt_rotary_keys, "head", axis=1, tiled=True),
        lax.all_gather(positions, "head", axis=0, tiled=True),
    )
    token_count = rows_query.shape[0]
    head_count = key_up_weight.shape[1] // D_NOPE
    queries = jnp.dot(rows_query, query_up_weight, preferred_element_type=jnp.float32).reshape(
        token_count, head_count, D_NOPE + D_ROPE
    )
    query_rope = rotate(queries[..., D_NOPE:], rows_place[:, None])
    queries = jnp.concatenate([queries[..., :D_NOPE], query_rope], axis=-1).astype(jnp.bfloat16)
    key_nope = (
        jnp.dot(rows_latent, key_up_weight, preferred_element_type=jnp.float32)
        .astype(jnp.bfloat16)
        .reshape(token_count, head_count, D_NOPE)
    )
    value_rows = (
        jnp.dot(rows_latent, value_up_weight, preferred_element_type=jnp.float32)
        .astype(jnp.bfloat16)
        .reshape(token_count, head_count, D_V)
    )
    key_rope = rotate(rows_rope.T.astype(jnp.float32), rows_place).astype(jnp.bfloat16)
    scores = (
        jnp.einsum(
            "shd,thd->hst", queries[..., :D_NOPE], key_nope, preferred_element_type=jnp.float32
        )
        + jnp.einsum(
            "shd,td->hst", queries[..., D_NOPE:], key_rope, preferred_element_type=jnp.float32
        )
    ) * score_scale
    token_index = jnp.arange(token_count, dtype=jnp.int32)
    visible = (token_index[None, :] <= token_index[:, None]) & (
        token_index[None, :] >= token_index[:, None] - rows_place[:, None]
    )
    scores = jnp.where(visible[None], scores, -jnp.inf)
    weights = jax.nn.softmax(scores, axis=-1).astype(jnp.bfloat16)
    attended = jnp.einsum(
        "hst,thd->shd", weights, value_rows, preferred_element_type=jnp.float32
    ).astype(jnp.bfloat16)
    return attended.reshape(token_count, head_count * D_V)


def attend(
    latent_query, query_rope, slot_ids, latent_cache_rows, rotated_cache_keys, cache_live_lengths
):
    score_scale = (D_NOPE + D_ROPE) ** (-0.5)
    safe_slots = jnp.clip(slot_ids, 0, latent_cache_rows.shape[0] - 1)
    latent = jnp.take(latent_cache_rows, safe_slots, axis=0)
    rope_rows = jnp.take(rotated_cache_keys, safe_slots, axis=0)
    length = jnp.take(cache_live_lengths, safe_slots, axis=0)
    scores = (
        jnp.einsum("nhc,ntc->nht", latent_query, latent, preferred_element_type=jnp.float32)
        + jnp.einsum("nhd,ndt->nht", query_rope, rope_rows, preferred_element_type=jnp.float32)
    ) * score_scale
    visible = jnp.arange(latent.shape[1], dtype=jnp.int32)[None, None, :] < length[:, None, None]
    scores = jnp.where(visible, scores, -jnp.inf)
    weights = jax.nn.softmax(scores, axis=-1).astype(jnp.bfloat16)
    return jnp.einsum("nht,ntc->nhc", weights, latent, preferred_element_type=jnp.float32).astype(
        jnp.bfloat16
    )


def absorb(query_nope, key_map):
    return jnp.einsum(
        "rhd,chd->rhc", query_nope, key_map, preferred_element_type=jnp.float32
    ).astype(jnp.bfloat16)


def decode(
    decode_queries,
    decode_owner_index,
    decode_cache_slot,
    latent_cache_rows,
    rotated_cache_keys,
    cache_live_lengths,
    key_up_weight,
    value_up_weight,
):
    row_count = decode_queries.shape[0]
    peer_count = lax.axis_size("req")
    slot_most = max(2, row_count * 2 // peer_count)
    head_count = key_up_weight.shape[1] // D_NOPE
    key_map = key_up_weight.reshape(D_C, head_count, D_NOPE)
    value_map = value_up_weight.reshape(D_C, head_count, D_V)
    row_index = jnp.arange(row_count, dtype=jnp.int32)
    earlier = (decode_owner_index[:, None] == decode_owner_index[None, :]) & (
        row_index[None, :] < row_index[:, None]
    )
    target = decode_owner_index * slot_most + jnp.sum(earlier.astype(jnp.int32), axis=1)
    placing = target[None, :] == jnp.arange(peer_count * slot_most, dtype=jnp.int32)[:, None]
    scatter_rows = placing.astype(jnp.bfloat16)
    slot_send = (
        jnp.sum(jnp.where(placing, decode_cache_slot[None, :] + 1, 0), axis=1) - 1
    ).reshape(peer_count, slot_most)
    queries = decode_queries.reshape(row_count, head_count, D_NOPE + D_ROPE)
    latent_query = absorb(queries[..., :D_NOPE], key_map)
    packed = jnp.concatenate([latent_query, queries[..., D_NOPE:]], axis=-1).reshape(
        row_count, head_count * (D_C + D_ROPE)
    )
    sending = (
        jnp.dot(scatter_rows, packed, preferred_element_type=jnp.float32)
        .astype(jnp.bfloat16)
        .reshape(peer_count, slot_most, head_count * (D_C + D_ROPE))
    )
    query_slots = lax.all_to_all(sending, "req", split_axis=0, concat_axis=0, tiled=True)
    slot_ids = lax.all_to_all(slot_send, "req", split_axis=0, concat_axis=0, tiled=True)
    item_count = slot_ids.shape[1]
    flattened = query_slots.reshape(peer_count * item_count, head_count, D_C + D_ROPE)
    latent_out = attend(
        flattened[..., :D_C],
        flattened[..., D_C:],
        slot_ids.reshape(-1),
        latent_cache_rows,
        rotated_cache_keys,
        cache_live_lengths,
    )
    returned = lax.all_to_all(
        latent_out.reshape(peer_count, item_count, head_count * D_C),
        "req",
        split_axis=0,
        concat_axis=0,
        tiled=True,
    )
    gathered = jnp.dot(
        scatter_rows.T,
        returned.reshape(peer_count * slot_most, head_count * D_C),
        preferred_element_type=jnp.float32,
    ).astype(jnp.bfloat16)
    result = jnp.einsum(
        "rhc,chd->rhd",
        gathered.reshape(row_count, head_count, D_C),
        value_map,
        preferred_element_type=jnp.float32,
    ).astype(jnp.bfloat16)
    result = result.reshape(row_count, head_count * D_V)
    return result


def on_device(
    prompt_query_latents,
    prompt_latents,
    prompt_rotary_keys,
    positions,
    query_up_weight,
    key_up_weight,
    value_up_weight,
    decode_queries,
    decode_owner_index,
    decode_cache_slot,
    latent_cache_rows,
    rotated_cache_keys,
    cache_live_lengths,
):
    prompt_attention_output = prompt_prefill(
        prompt_query_latents,
        prompt_latents,
        prompt_rotary_keys,
        positions,
        query_up_weight,
        key_up_weight,
        value_up_weight,
    )
    decode_out = decode(
        decode_queries,
        decode_owner_index,
        decode_cache_slot,
        latent_cache_rows,
        rotated_cache_keys,
        cache_live_lengths,
        key_up_weight,
        value_up_weight,
    )
    return (prompt_attention_output, decode_out)


def solution(mesh):
    placed = (
        P(("req", "head"), None),
        P(("req", "head"), None),
        P(None, ("req", "head")),
        P(("req", "head")),
        P(None, "head"),
        P(None, "head"),
        P(None, "head"),
        P("req", "head"),
        P("req"),
        P("req"),
        P("req", None, None),
        P("req", None, None),
        P("req"),
    )
    return jax.shard_map(
        on_device,
        mesh=mesh,
        in_specs=placed,
        out_specs=(P("req", "head"), P("req", "head")),
        check_vma=False,
    )
```

profile of v0, /device:TPU:0, one launch (start us, length us, event | category | flops | bytes accessed | tf_op | source)
XLA Modules:
  0.0 204.0 jit_solution(16149366200486652376)
XLA Ops:
  9.7 7.3 %all-to-all-start = ((s32[8,1,16]{2,1,0:T(1,128)}), s32[8,1,16]{2,1,0:T(1,128)S(1)}, u32[]{:S(2)}, u32[]{:S(2)}) async-start(s32[8,1,16]{2,1,0:T(1,128)} %bitcast.9), calls=%async_computation | async-start | bytes 8192 | tf_op jit(solution)/shard_map/all_to_all | solution.py:149
  18.7 2.4 %fusion.28 = bf16[64,16,512]{2,0,1:T(8,128)(2,1)S(1)} fusion(bf16[64,16,128]{2,1,0:T(8,128)(2,1)S(1)} %slice.54, bf16[512,2048]{1,0:T(8,128)(2,1)} %param.18), kind=kOutput, calls=%fused_computation.39 | convolution fusion | flops 134742016 | bytes 3407872 | tf_op jit(solution)/shard_map/rhd,chd->rhc/dot_general | solution.py:107
  24.0 3.6 %convolution_convert_fusion = bf16[128,9216]{1,0:T(8,128)(2,1)} fusion(bf16[64,9216]{1,0:T(8,128)(2,1)} %reshape.250, s32[64]{0:T(128)S(1)} %get-tuple-element.24), kind=kOutput, calls=%fused_computation.13 | convolution fusion | flops 152182784 | bytes 3539200 | tf_op jit(solution)/shard_map/dot_general | solution.py:144
  27.6 6.1 %all-to-all-start.1 = ((bf16[8,16,9216]{2,1,0:T(8,128)(2,1)}), bf16[8,16,9216]{2,1,0:T(8,128)(2,1)}, u32[]{:S(2)}, u32[]{:S(2)}) async-start(bf16[8,16,9216]{2,1,0:T(8,128)(2,1)} %bitcast.74), calls=%async_computation.1 | async-start | bytes 4718592 | tf_op jit(solution)/shard_map/all_to_all | solution.py:148
  34.5 5.0 %all-gather = s32[4,1,128]{2,1,0:T(1,128)S(1)} all-gather(s32[1,1,128]{2,1,0:T(1,128)S(1)} %bitcast.85), channel_id=1, replica_groups=mesh['req'=8,'head'=4] {'head'}, dimensions={0}, use_global_device_ids=true | all-gather | bytes 2560 | tf_op jit(solution)/shard_map/all_gather | solution.py:46
  39.5 7.2 %all_gather.12 = bf16[512,512]{1,0:T(8,128)(2,1)S(1)} all-gather(bf16[128,512]{1,0:T(8,128)(2,1)S(1)} %copy-done.3), channel_id=1, replica_groups=mesh['req'=8,'head'=4] {'head'}, dimensions={0}, use_global_device_ids=true | all-gather | bytes 655360 | tf_op jit(solution)/shard_map/all_gather | solution.py:44
  46.7 4.2 %convolution_convert_fusion.3 = bf16[512,2048]{1,0:T(8,128)(2,1)} fusion(bf16[512,512]{1,0:T(8,128)(2,1)S(1)} %all_gather.12, bf16[512,2048]{1,0:T(8,128)(2,1)} %param.19), kind=kOutput, calls=%fused_computation.21 | convolution fusion | flops 1074790400 | bytes 4718592 | tf_op jit(solution)/shard_map/dot_general | solution.py:61
  50.9 3.9 %copy.83 = bf16[512,2048]{0,1:T(8,128)(2,1)} copy(bf16[512,2048]{1,0:T(8,128)(2,1)} %convolution_convert_fusion.3) | data formatting | bytes 4194304 | tf_op jit(solution)/shard_map/reshape | solution.py:63
  54.9 5.4 %all_gather.15 = bf16[64,512]{1,0:T(8,128)(2,1)S(1)} all-gather(bf16[64,128]{1,0:T(8,128)(2,1)S(1)} %copy-done.4), channel_id=1, replica_groups=mesh['req'=8,'head'=4] {'head'}, dimensions={1}, use_global_device_ids=true | all-gather | bytes 81920 | tf_op jit(solution)/shard_map/all_gather | solution.py:45
  60.9 4.2 %fusion.24 = bf16[64,16,8,128]{3,2,1,0:T(8,128)(2,1)} fusion(bf16[512,512]{1,0:T(8,128)(2,1)S(1)} %all_gather.12, bf16[512,2048]{1,0:T(8,128)(2,1)} %param.18), kind=kOutput, calls=%fused_computation.37 | convolution fusion | flops 1074790400 | bytes 4718592 | tf_op jit(solution)/shard_map/dot_general | solution.py:56
  66.5 2.9 %gather_fusion.2 = bf16[128,64,256]{2,1,0:T(8,128)(2,1)} fusion(bf16[64,64,256]{2,1,0:T(8,128)(2,1)S(1)} %copy-done, s32[1024]{0:T(1024)S(1)} %pad_clamp_fusion), kind=kCustom, calls=%fused_computation.2 | custom fusion | bytes 8389120 | tf_op jit(solution)/shard_map/jit(_take)/gather | solution.py:92
  69.4 18.3 %gather_fusion.1 = bf16[128,256,512]{2,1,0:T(8,128)(2,1)} fusion(bf16[64,256,512]{2,1,0:T(8,128)(2,1)} %param.23, s32[1024]{0:T(1024)S(1)} %pad_clamp_fusion), kind=kCustom, calls=%fused_computation.1 | custom fusion | bytes 67109376 | tf_op jit(solution)/shard_map/jit(_take)/gather | solution.py:91
  87.8 5.1 %reshape.252 = bf16[128,16,576]{2,1,0:T(8,128)(2,1)} reshape(bf16[8,16,9216]{2,1,0:T(8,128)(2,1)} %all-to-all-done.1) | data formatting | bytes 4718592 | tf_op jit(solution)/shard_map/reshape | solution.py:151
  92.8 3.2 %fusion.7 = f32[128,16,256]{2,1,0:T(8,128)S(1)} fusion(bf16[128,64,256]{2,1,0:T(8,128)(2,1)} %gather_fusion.2, pred[128]{0:T(512)(128)(4,1)S(1)} %get-tuple-element.13, bf16[128,16,576]{2,1,0:T(8,128)(2,1)} %reshape.252), kind=kOutput, calls=%fused_computation.17 | convolution fusion | flops 69206016 | bytes 6815872 | tf_op jit(solution)/shard_map/nhd,ndt->nht/dot_general | solution.py:96
  96.0 16.8 %fusion.60 = (f32[128,16]{1,0:T(8,128)S(1)}, f32[128,16,256]{2,1,0:T(8,128)}) fusion(f32[128,16,256]{2,1,0:T(8,128)S(1)} %fusion.7, bf16[128,256,512]{2,1,0:T(8,128)(2,1)} %gather_fusion.1, pred[128]{0:T(512)(128)(4,1)S(1)} %get-tuple-element.13, bf16[128,16,576]{2,1,0:T(8,128)(2,1)} %reshape.252, pred[128,256]{1,0:T(8,128)(4,1)S(1)} %iota_compare_fusion.2), kind=kOutput, calls=%fused_computation.93 | convolution fusion | flops 556269824 | bytes 39886976 | tf_op jit(solution)/shard_map/sub | solution.py:100
  112.8 13.9 %fusion.20 = bf16[128,16,512]{2,1,0:T(8,128)(2,1)S(1)} fusion(bf16[128,256,512]{2,1,0:T(8,128)(2,1)} %gather_fusion.1, pred[128]{0:T(512)(128)(4,1)S(1)} %get-tuple-element.13, f32[128,16,256]{2,1,0:T(8,128)} %get-tuple-element.23, f32[128,16]{1,0:T(8,128)S(1)} %get-tuple-element.22), kind=kOutput, calls=%fused_computation.35 | convolution fusion | flops 555745280 | bytes 37757056 | tf_op jit(solution)/shard_map/nht,ntc->nhc/dot_general | solution.py:101
  126.7 2.4 %reshape.253 = bf16[8,16,8192]{2,1,0:T(8,128)(2,1)} reshape(bf16[128,16,512]{2,1,0:T(8,128)(2,1)S(1)} %fusion.20) | data formatting | bytes 4194304 | tf_op jit(solution)/shard_map/reshape | solution.py:161
  129.1 6.2 %all-to-all-start.2 = ((bf16[8,16,8192]{2,1,0:T(8,128)(2,1)}), bf16[8,16,8192]{2,1,0:T(8,128)(2,1)S(1)}, u32[]{:S(2)}, u32[]{:S(2)}) async-start(bf16[8,16,8192]{2,1,0:T(8,128)(2,1)} %reshape.253), calls=%async_computation.2 | async-start | bytes 4194304 | tf_op jit(solution)/shard_map/all_to_all | solution.py:160
  135.3 8.3 %fusion.63 = f32[512,3072]{0,1:T(8,128)S(1)} fusion(bf16[512,1536]{1,0:T(8,128)(2,1)} %all-gather.3.cloned.1.call-done, bf16[1536,3072]{1,0:T(8,128)(2,1)} %param.17), kind=kOutput, calls=%fused_computation.94 | convolution fusion | flops 4831838208 | bytes 17301504 | tf_op jit(solution)/shard_map/dot_general | solution.py:50
  144.1 8.1 %fusion.39 = f32[512,512,16]{1,0,2:T(8,128)} fusion(bf16[512,16,32]{0,2,1:T(8,128)(2,1)S(1)} %get-tuple-element.15, bf16[512,16,32]{0,2,1:T(8,128)(2,1)S(1)} %get-tuple-element.14, bf16[512,32]{0,1:T(8,128)(2,1)S(1)} %get-tuple-element.17, bf16[512,32]{0,1:T(8,128)(2,1)S(1)} %get-tuple-element.16), kind=kOutput, calls=%fused_computation.45 | convolution fusion | flops 539099136 | bytes 17891328 | tf_op jit(solution)/shard_map/shd,td->hst/dot_general | solution.py:70
  152.1 11.5 %fusion.3 = f32[16,512,512]{1,2,0:T(8,128)} fusion(f32[512,512,16]{1,0,2:T(8,128)} %fusion.39, pred[512,512]{0,1:T(8,128)(4,1)S(1)} %fusion.44, f32[512,16,192]{0,2,1:T(8,128)S(1)} %bitcast.77, bf16[64,16,8,128]{3,2,1,0:T(8,128)(2,1)} %fusion.24), kind=kOutput, calls=%fused_computation.8 | convolution fusion | flops 1086324736 | bytes 38010880 | tf_op jit(solution)/shard_map/shd,thd->hst/dot_general | solution.py:67
  163.6 12.0 %fusion.59 = f32[16,512]{1,0:T(8,128)S(1)} fusion(f32[16,512,512]{1,2,0:T(8,128)} %fusion.3), kind=kOutput, calls=%fused_computation.92 | output fusion | flops 8389119 | bytes 16809984 | tf_op jit(solution)/shard_map/sub | solution.py:79
  175.6 14.7 %fusion.21 = bf16[16,128,512]{2,1,0:T(8,128)(2,1)} fusion(bf16[512,16,128]{0,2,1:T(8,128)(2,1)} %bitcast.78, f32[16,512]{1,0:T(8,128)S(1)} %fusion.59, f32[16,512,512]{1,2,0:T(8,128)} %fusion.3), kind=kOutput, calls=%fused_computation.36 | convolution fusion | flops 1087382016 | bytes 21004288 | tf_op jit(solution)/shard_map/hst,thd->shd/dot_general | solution.py:80
  190.4 3.9 %copy.79 = bf16[512,2048]{1,0:T(8,128)(2,1)} copy(bf16[512,2048]{0,1:T(8,128)(2,1)} %bitcast.79) | data formatting | bytes 4194304
  (50 shorter events, 13.1 us)
Async XLA Ops:
  7.2 59.3 %copy-start = (bf16[64,64,256]{2,1,0:T(8,128)(2,1)S(1)}, bf16[64,64,256]{2,1,0:T(8,128)(2,1)}, u32[]{:S(2)}) copy-start(bf16[64,64,256]{2,1,0:T(8,128)(2,1)} %param.24) | copy-start | bytes 6291460
  9.7 17.9 %all-to-all-start = ((s32[8,1,16]{2,1,0:T(1,128)}), s32[8,1,16]{2,1,0:T(1,128)S(1)}, u32[]{:S(2)}, u32[]{:S(2)}) async-start(s32[8,1,16]{2,1,0:T(1,128)} %bitcast.9), calls=%async_computation | async-start | bytes 8192 | tf_op jit(solution)/shard_map/all_to_all | solution.py:149
  27.6 6.9 %copy-start.5 = (s32[128]{0:T(128)S(1)}, s32[128]{0:T(128)}, u32[]{:S(2)}) copy-start(s32[128]{0:T(128)} %param.16) | copy-start | bytes 1540
  27.6 11.9 %copy-start.3 = (bf16[128,512]{1,0:T(8,128)(2,1)S(1)}, bf16[128,512]{1,0:T(8,128)(2,1)}, u32[]{:S(2)}) copy-start(bf16[128,512]{1,0:T(8,128)(2,1)} %param.14) | copy-start | bytes 393220
  27.6 60.2 %all-to-all-start.1 = ((bf16[8,16,9216]{2,1,0:T(8,128)(2,1)}), bf16[8,16,9216]{2,1,0:T(8,128)(2,1)}, u32[]{:S(2)}, u32[]{:S(2)}) async-start(bf16[8,16,9216]{2,1,0:T(8,128)(2,1)} %bitcast.74), calls=%async_computation.1 | async-start | bytes 4718592 | tf_op jit(solution)/shard_map/all_to_all | solution.py:148
  33.7 101.6 %all-gather.3.cloned.1.call-start = ((), (), s32[]{:S(2)}) async-start(), calls=%async_computation.3 | async-start | bytes 1966080 | tf_op jit(solution)/shard_map/all_gather | solution.py:43
  50.9 4.0 %copy-start.4 = (bf16[64,128]{1,0:T(8,128)(2,1)S(1)}, bf16[64,128]{1,0:T(8,128)(2,1)}, u32[]{:S(2)}) copy-start(bf16[64,128]{1,0:T(8,128)(2,1)} %param.15) | copy-start | bytes 49156
  60.8 4.4 %copy-start.2 = (s32[64]{0:T(128)S(1)}, s32[64]{0:T(128)}, u32[]{:S(2)}) copy-start(s32[64]{0:T(128)} %param.25) | copy-start | bytes 772
  129.1 65.1 %all-to-all-start.2 = ((bf16[8,16,8192]{2,1,0:T(8,128)(2,1)}), bf16[8,16,8192]{2,1,0:T(8,128)(2,1)S(1)}, u32[]{:S(2)}, u32[]{:S(2)}) async-start(bf16[8,16,8192]{2,1,0:T(8,128)(2,1)} %reshape.253), calls=%async_computation.2 | async-start | bytes 4194304 | tf_op jit(solution)/shard_map/all_to_all | solution.py:160
  194.3 1.6 copy-start.6
  194.8 2.4 %copy-start.1 = (bf16[64,64,256]{2,1,0:T(8,128)(2,1)S(1)}, bf16[64,64,256]{2,1,0:T(8,128)(2,1)}, u32[]{:S(2)}) copy-start(bf16[64,64,256]{2,1,0:T(8,128)(2,1)} %param.24) | copy-start | bytes 6291460
Sparse Core Ops, SparseCore 0:
  36.1 21.0 all-gather.2
where the time goes:
time: 205 us; the launch traced here: 204 us
  matrix products  92 us (45%)
  local copies, waits for them, and re-layouts  44.9 us (22%)
  starting transfers between devices  19.6 us (10%)
  blocking collectives  17.7 us (9%)
  other arithmetic  14.9 us (7%)
  between operations  14.2 us (7%)
    gather x1, local copies, waits for them, and re-layouts, attend(): latent = jnp.take(latent_cache_rows, safe_slots, axis=0)  18.3 us
    sub x1, matrix products, attend(): weights = jax.nn.softmax(scores, axis=-1).astype(jnp.bfloat16)  16.8 us
    dot_general x1, matrix products, prompt_prefill(): jnp.einsum('hst,thd->shd', weights, value_rows, preferred_element_type=jn...  14.7 us
    dot_general x1, matrix products, attend(): jnp.einsum('nht,ntc->nhc', weights, latent, preferred_element_type=jnp.fl...  13.9 us
    sub x1, other arithmetic, prompt_prefill(): weights = jax.nn.softmax(scores, axis=-1).astype(jnp.bfloat16)  12 us
    dot_general x1, matrix products, prompt_prefill(): jnp.einsum('shd,thd->hst', queries[..., :D_NOPE], key_nope, preferred_ele...  11.5 us
    dot_general x1, matrix products, prompt_prefill(): jnp.dot(rows_query, query_up_weight, preferred_element_type=jnp.float32)  8.35 us
    dot_general x1, matrix products, prompt_prefill(): jnp.einsum('shd,td->hst', queries[..., D_NOPE:], key_rope, preferred_elem...  8.09 us
  transfers between devices with their start and end apart: 4, of which 0 were waited for; matrix products, arithmetic and copies ran while one was open for 72% of the time, Pallas kernels for 0%

commit v1 on v0

v1 whole, which is shorter than its diff:
```python
import functools
import math

import jax
import jax.numpy as jnp
from jax import lax
from jax.experimental import pallas as pl
from jax.experimental.pallas import tpu as pltpu
from jax.sharding import PartitionSpec as P

D_C = 512
D_NOPE = 128
D_ROPE = 64
D_V = 128
D_Q = D_NOPE + D_ROPE
ROPE_BASE = 10000.0
SCALE = D_Q ** (-0.5)
EXP2_SCALE = SCALE * math.log2(math.e)
MASKED = -1e30
DIGIT = 256
NT = (((1,), (1,)), ((), ()))
TN = (((0,), (0,)), ((), ()))
VMEM_BYTES = 56 * 1024 * 1024


def mm(a, b, dims=(((1,), (0,)), ((), ()))):
    return lax.dot_general(a, b, dims, preferred_element_type=jnp.float32)


def softmax_weights(scores):
    shifted = scores - jnp.max(scores, axis=-1, keepdims=True)
    grown = jnp.exp2(shifted * EXP2_SCALE)
    total = jnp.sum(grown, axis=-1, keepdims=True)
    return (grown * (1.0 / total)).astype(jnp.bfloat16)


def decode_kernel(
    slots_per_step,
    head_count,
    lengths_ref,
    payload_ref,
    key_up_ref,
    value_up_ref,
    cache_ref,
    rope_ref,
    out_ref,
    nope_ref,
    rope_query_ref,
):
    step = pl.program_id(0)
    width = head_count * D_Q
    slot_count = nope_ref.shape[0]
    rows = slots_per_step * head_count

    @pl.when(step == 0)
    def _():
        requests = payload_ref.shape[0]
        owner = payload_ref[:, width : width + 1].astype(jnp.float32)
        slot = payload_ref[:, width + 1 : width + 2].astype(jnp.float32)
        me = lax.axis_index("req").astype(jnp.float32)
        lanes = lax.broadcasted_iota(jnp.int32, (requests, slot_count), 1).astype(jnp.float32)
        chosen = jnp.where((owner == me) & (slot == lanes), 1.0, 0.0).astype(jnp.bfloat16)
        for head in range(head_count):
            columns = mm(chosen, payload_ref[:, head * D_Q : (head + 1) * D_Q], TN)
            nope_ref[:, head * D_NOPE : (head + 1) * D_NOPE] = columns[:, :D_NOPE]
            rope_query_ref[:, head * D_ROPE : (head + 1) * D_ROPE] = columns[:, D_NOPE:]

    first = pl.multiple_of(step * slots_per_step, slots_per_step)

    def spread(values, unit):
        shape = (slots_per_step, head_count, head_count * unit)
        own = lax.broadcasted_iota(jnp.int32, shape, 1) == (
            lax.broadcasted_iota(jnp.int32, shape, 2) // unit
        )
        wide = jnp.where(own, jnp.broadcast_to(values[:, None, :], shape), 0.0)
        return wide.reshape(rows, head_count * unit).astype(jnp.bfloat16), own

    nope, own_head = spread(nope_ref[pl.ds(first, slots_per_step), :], D_NOPE)
    latent_query = mm(nope, key_up_ref[...], NT).astype(jnp.bfloat16)
    ropes, _ = spread(rope_query_ref[pl.ds(first, slots_per_step), :], D_ROPE)
    fold = (
        lax.broadcasted_iota(jnp.int32, (head_count * D_ROPE, D_ROPE), 0) % D_ROPE
        == lax.broadcasted_iota(jnp.int32, (head_count * D_ROPE, D_ROPE), 1)
    )
    rope_query = mm(ropes, jnp.where(fold, 1.0, 0.0).astype(jnp.bfloat16)).astype(jnp.bfloat16)

    lanes = lax.broadcasted_iota(jnp.int32, (head_count, cache_ref.shape[1]), 1)
    parts = []
    for item in range(slots_per_step):
        latent = cache_ref[item]
        place = slice(item * head_count, (item + 1) * head_count)
        scores = mm(latent_query[place], latent, NT) + mm(rope_query[place], rope_ref[item])
        scores = jnp.where(lanes < lengths_ref[first + item], scores, MASKED)
        parts.append(mm(softmax_weights(scores), latent).astype(jnp.bfloat16))
    latent_out = jnp.concatenate(parts, axis=0)
    raised = mm(latent_out, value_up_ref[...]).reshape(
        slots_per_step, head_count, head_count * D_V
    )
    out_ref[...] = jnp.sum(jnp.where(own_head, raised, 0.0), axis=1).astype(jnp.bfloat16)


def decode_attention(payload, key_up, value_up, cache, rope_cache, lengths):
    slot_count, cache_rows, _ = cache.shape
    head_count = key_up.shape[1] // D_NOPE
    per_step = 8
    whole = lambda step, *_: (0, 0)
    flops = 2 * slot_count * head_count * (
        2 * head_count * D_NOPE * D_C + 2 * cache_rows * D_C + cache_rows * D_ROPE
    )
    return pl.pallas_call(
        functools.partial(decode_kernel, per_step, head_count),
        out_shape=jax.ShapeDtypeStruct((slot_count, head_count * D_V), jnp.bfloat16),
        grid_spec=pltpu.PrefetchScalarGridSpec(
            num_scalar_prefetch=1,
            grid=(slot_count // per_step,),
            in_specs=[
                pl.BlockSpec(payload.shape, whole),
                pl.BlockSpec(key_up.shape, whole),
                pl.BlockSpec(value_up.shape, whole),
                pl.BlockSpec((per_step, cache_rows, D_C), lambda step, *_: (step, 0, 0)),
                pl.BlockSpec((per_step, D_ROPE, cache_rows), lambda step, *_: (step, 0, 0)),
            ],
            out_specs=pl.BlockSpec((per_step, head_count * D_V), lambda step, *_: (step, 0)),
            scratch_shapes=[
                pltpu.VMEM((slot_count, head_count * D_NOPE), jnp.float32),
                pltpu.VMEM((slot_count, head_count * D_ROPE), jnp.float32),
            ],
        ),
        compiler_params=pltpu.CompilerParams(vmem_limit_bytes=VMEM_BYTES),
        cost_estimate=pl.CostEstimate(
            flops=flops, bytes_accessed=cache.size * 2 + payload.size * 2, transcendentals=0
        ),
    )(lengths, payload, key_up, value_up, cache, rope_cache)


def prefill_kernel(
    query_latents_ref,
    latents_ref,
    extras_ref,
    cosines_ref,
    sines_ref,
    query_up_ref,
    key_up_ref,
    value_up_ref,
    out_ref,
    bias_ref,
    key_rope_ref,
):
    tokens = query_latents_ref.shape[0]
    lanes = lax.broadcasted_iota(jnp.int32, (tokens, D_NOPE), 1)
    low = lanes < D_ROPE

    def rotated(values):
        swapped = jnp.where(
            lanes % D_ROPE < D_ROPE // 2,
            pltpu.roll(values, D_NOPE - D_ROPE // 2, 1),
            pltpu.roll(values, D_ROPE // 2, 1),
        )
        return values * cosines_ref[...] + swapped * sines_ref[...]

    @pl.when(pl.program_id(0) == 0)
    def _():
        extras = extras_ref[...].astype(jnp.float32)
        position = extras[:, D_ROPE : D_ROPE + 1] * DIGIT + extras[:, D_ROPE + 1 : D_ROPE + 2]
        row = lax.broadcasted_iota(jnp.int32, (tokens, tokens), 0).astype(jnp.float32)
        column = lax.broadcasted_iota(jnp.int32, (tokens, tokens), 1).astype(jnp.float32)
        visible = (column <= row) & (column >= row - position)
        bias_ref[...] = jnp.where(visible, 0.0, MASKED)
        twice = jnp.where(low, extras, pltpu.roll(extras, D_ROPE, 1))
        key_rope_ref[...] = rotated(twice).astype(jnp.bfloat16)

    projected = mm(query_latents_ref[...], query_up_ref[...])
    left = projected[:, :D_NOPE].astype(jnp.bfloat16)
    middle = projected[:, D_NOPE : 2 * D_NOPE]
    middle = jnp.where(low, rotated(middle), middle).astype(jnp.bfloat16)
    right = projected[:, 2 * D_NOPE :]
    right = jnp.where(low, right, rotated(right)).astype(jnp.bfloat16)
    keys = mm(latents_ref[...], key_up_ref[...])
    values = mm(latents_ref[...], value_up_ref[...]).astype(jnp.bfloat16)
    key_rope = key_rope_ref[...].astype(jnp.float32)
    turned = pltpu.roll(keys[:, D_NOPE:], D_ROPE, 1)
    pairs = (
        (
            jnp.concatenate([left, middle], axis=1),
            jnp.concatenate([keys[:, :D_NOPE], jnp.where(low, key_rope, 0.0)], axis=1),
        ),
        (
            jnp.concatenate([middle, right], axis=1),
            jnp.concatenate(
                [jnp.where(low, 0.0, turned), jnp.where(low, turned, key_rope)], axis=1
            ),
        ),
    )
    tile = 128
    for head, (query, key) in enumerate(pairs):
        key = key.astype(jnp.bfloat16)
        value = values[:, head * D_V : (head + 1) * D_V]
        for begin in range(0, tokens, tile):
            end = begin + tile
            scores = mm(query[begin:end], key[:end], NT) + bias_ref[begin:end, :end]
            weights = softmax_weights(scores)
            out_ref[begin:end, head * D_V : (head + 1) * D_V] = mm(weights, value[:end]).astype(
                jnp.bfloat16
            )


def prefill_attention(gathered, cosines, sines, query_up, key_up, value_up):
    tokens = gathered.shape[0]
    latent_width = query_up.shape[0]
    head_count = key_up.shape[1] // D_NOPE
    extra_block = (latent_width + D_C) // D_NOPE
    whole = lambda step: (0, 0)
    across = lambda step: (0, step)
    flops = 2 * tokens * head_count * (latent_width * D_Q + 2 * D_C * D_NOPE + tokens * 384)
    return pl.pallas_call(
        prefill_kernel,
        out_shape=jax.ShapeDtypeStruct((tokens, head_count * D_V), jnp.bfloat16),
        grid=(head_count // 2,),
        in_specs=[
            pl.BlockSpec((tokens, latent_width), whole),
            pl.BlockSpec((tokens, D_C), lambda step: (0, latent_width // D_C)),
            pl.BlockSpec((tokens, D_NOPE), lambda step: (0, extra_block)),
            pl.BlockSpec((tokens, D_NOPE), whole),
            pl.BlockSpec((tokens, D_NOPE), whole),
            pl.BlockSpec((latent_width, 2 * D_Q), across),
            pl.BlockSpec((D_C, 2 * D_NOPE), across),
            pl.BlockSpec((D_C, 2 * D_V), across),
        ],
        out_specs=pl.BlockSpec((tokens, 2 * D_V), across),
        scratch_shapes=[
            pltpu.VMEM((tokens, tokens), jnp.float32),
            pltpu.VMEM((tokens, D_NOPE), jnp.bfloat16),
        ],
        compiler_params=pltpu.CompilerParams(vmem_limit_bytes=VMEM_BYTES),
        cost_estimate=pl.CostEstimate(
            flops=flops, bytes_accessed=query_up.size * 2 + key_up.size * 4, transcendentals=0
        ),
    )(gathered, gathered, gathered, cosines, sines, query_up, key_up, value_up)


def rope_tables(position):
    half_width = D_ROPE // 2
    frequency = ROPE_BASE ** (-jnp.arange(half_width, dtype=jnp.float32) / half_width)
    angles = position.astype(jnp.float32)[:, None] * frequency
    cosines, sines = jnp.cos(angles), jnp.sin(angles)
    return (
        jnp.concatenate([cosines] * 4, axis=1),
        jnp.concatenate([-sines, sines] * 2, axis=1),
    )


def on_device(
    prompt_query_latents,
    prompt_latents,
    prompt_rotary_keys,
    positions,
    query_up_weight,
    key_up_weight,
    value_up_weight,
    decode_queries,
    decode_owner_index,
    decode_cache_slot,
    latent_cache_rows,
    rotated_cache_keys,
    cache_live_lengths,
):
    row_count = decode_queries.shape[0]
    slot_count = latent_cache_rows.shape[0]
    token_count = prompt_latents.shape[0]

    def digits(first, second, rows, width):
        lane = lax.broadcasted_iota(jnp.int32, (rows, width), 1)
        return jnp.where(
            lane == 0, first[:, None], jnp.where(lane == 1, second[:, None], 0)
        ).astype(jnp.bfloat16)

    payload = jnp.concatenate(
        [decode_queries, digits(decode_owner_index, decode_cache_slot, row_count, 128)], axis=1
    )
    payload = lax.all_gather(payload, "req", axis=0, tiled=True)
    prompt = jnp.concatenate(
        [
            prompt_query_latents,
            prompt_latents,
            prompt_rotary_keys.T,
            digits(positions // DIGIT, positions % DIGIT, token_count, 64),
        ],
        axis=1,
    )
    prompt = lax.all_gather(prompt, "head", axis=0, tiled=True)

    answers = decode_attention(
        payload,
        key_up_weight,
        value_up_weight,
        latent_cache_rows,
        rotated_cache_keys,
        cache_live_lengths,
    )
    returned = lax.all_gather(answers, "req", axis=0, tiled=True)
    prompt, answers = lax.optimization_barrier((prompt, answers))

    place = prompt_query_latents.shape[1] + D_C + D_ROPE
    high_low = prompt[:, place : place + 2].astype(jnp.int32)
    cosines, sines = rope_tables(high_low[:, 0] * DIGIT + high_low[:, 1])
    prompt_attention_output = prefill_attention(
        prompt, cosines, sines, query_up_weight, key_up_weight, value_up_weight
    )
    cache_index = decode_owner_index * slot_count + decode_cache_slot
    wanted = (
        cache_index[:, None] == jnp.arange(returned.shape[0], dtype=jnp.int32)[None, :]
    ).astype(jnp.bfloat16)
    decode_out = jnp.dot(wanted, returned, preferred_element_type=jnp.float32).astype(
        jnp.bfloat16
    )
    return (prompt_attention_output, decode_out)


def solution(mesh):
    placed = (
        P(("req", "head"), None),
        P(("req", "head"), None),
        P(None, ("req", "head")),
        P(("req", "head")),
        P(None, "head"),
        P(None, "head"),
        P(None, "head"),
        P("req", "head"),
        P("req"),
        P("req"),
        P("req", None, None),
        P("req", None, None),
        P("req"),
    )
    return jax.shard_map(
        on_device,
        mesh=mesh,
        in_specs=placed,
        out_specs=(P("req", "head"), P("req", "head")),
        check_vma=False,
    )
```

time: 205 us -> 177 us (0.86)
  matrix products: 92 us -> 2.81 us
  Pallas kernels: 0 us -> 78.2 us
  waiting for transfers between devices: 0.7 us -> 72 us
  local copies, waits for them, and re-layouts: 44.9 us -> 2.7 us
  starting transfers between devices: 19.6 us -> 0.12 us
  blocking collectives: 17.7 us -> 0 us
  other arithmetic: 14.9 us -> 7.51 us
    pallas_call x0 -> x2, Pallas kernels: none -> 78.2 us  [the longest x1 44.7 us: decode_attention(): pl.pallas_call(functools.partial(decode_kernel, per_step, head_count), ou...]
    dot_general x12 -> x1, matrix products: 75.1 us -> 2.81 us  [on_device(): jnp.dot(wanted, returned, preferred_element_type=jnp.float32)]
    all_gather x1 -> x3, waiting for transfers between devices: 0.01 us -> 71.9 us  [the longest x1 61.5 us: on_device(): payload = lax.all_gather(payload, 'req', axis=0, tiled=True)]
    gather x3 -> x0, local copies, waits for them, and re-layouts: 22.4 us -> none  [the longest x1 18.3 us: attend(): latent = jnp.take(latent_cache_rows, safe_slots, axis=0)]
    all_to_all x3 -> x0, starting transfers between devices: 19.6 us -> none  [the longest x1 7.25 us: decode(): lax.all_to_all(slot_send, 'req', split_axis=0, concat_axis=0, tiled=True)]
    all_gather x3 -> x0, blocking collectives: 17.7 us -> none  [the longest x1 7.23 us: prompt_prefill(): lax.all_gather(prompt_latents, 'head', axis=0, tiled=True)]
    sub x1 -> x0, matrix products: 16.8 us -> none  [attend(): weights = jax.nn.softmax(scores, axis=-1).astype(jnp.bfloat16)]
    reshape x6 -> x0, local copies, waits for them, and re-layouts: 15.7 us -> none  [the longest x1 5.05 us: decode(): query_slots.reshape(peer_count * item_count, head_count, D_C + D_ROPE)]
  transfers between devices with their start and end apart: 4 -> 3, of which waited for: 0 -> 2; matrix products, arithmetic and copies ran while one was open for 72% -> 4% of each run, Pallas kernels for 0% -> 44%
where the time goes in v1:
time: 177 us
  Pallas kernels  78.2 us (44%)
  waiting for transfers between devices  72 us (41%)
  between operations  13.8 us (8%)
  other arithmetic  7.51 us (4%)
  matrix products  2.81 us (2%)
  local copies, waits for them, and re-layouts  2.7 us (2%)
    all_gather x1, waiting for transfers between devices, on_device(): payload = lax.all_gather(payload, 'req', axis=0, tiled=True)  61.5 us
    pallas_call x1, Pallas kernels, decode_attention(): pl.pallas_call(functools.partial(decode_kernel, per_step, head_count), ou...  44.7 us
    pallas_call x1, Pallas kernels, prefill_attention(): pl.pallas_call(prefill_kernel, out_shape=jax.ShapeDtypeStruct((tokens, he...  33.4 us
    all_gather x1, waiting for transfers between devices, on_device(): returned = lax.all_gather(answers, 'req', axis=0, tiled=True)  10.4 us
  transfers between devices with their start and end apart: 3, of which 2 were waited for; matrix products, arithmetic and copies ran while one was open for 4% of the time, Pallas kernels for 44%

profile of v1, /device:TPU:0, one launch (start us, length us, event | category | flops | bytes accessed | tf_op | source)
XLA Modules:
  0.0 177.1 jit_solution(2489590563066860800)
XLA Ops:
  7.2 0.0 all-gather.6.cloned.1.call-start
  7.2 0.8 select_convert_fusion.1
  8.0 1.8 %pad_maximum_fusion = bf16[64,3200]{1,0:T(8,128)(2,1)} fusion(bf16[64,128]{1,0:T(8,128)(2,1)S(1)} %select_convert_fusion.1, bf16[64,3072]{1,0:T(8,128)(2,1)} %param.20), kind=kLoop, calls=%fused_computation.1 | loop fusion | flops 819200 | bytes 819200 | tf_op jit(solution)/shard_map/concatenate | solution.py:277
  9.8 0.0 all-gather.6.cloned.1.call-update
  9.8 0.0 all-gather.4.cloned.1.call-start
  9.8 0.8 copy.17
  10.7 0.7 and_select_fusion.1
  11.3 0.1 select_convert_fusion
  11.5 1.9 %concatenate.12 = bf16[128,2176]{1,0:T(8,128)(2,1)} concatenate(bf16[128,1536]{1,0:T(8,128)(2,1)} %param.13, bf16[128,512]{1,0:T(8,128)(2,1)} %param.14, bf16[128,64]{1,0:T(8,128)(2,1)S(1)} %bitcast.2, bf16[128,64]{1,0:T(8,128)(2,1)S(1)} %select_convert_fusion), dimensions={1} | concatenate | bytes 1114112 | tf_op jit(solution)/shard_map/concatenate | solution.py:281
  13.3 0.0 all-gather.4.cloned.1.call-update
  13.3 0.0 copy-start.1
  13.4 0.0 all-gather.8.cloned.1.call-start
  13.4 61.5 %all-gather.6.cloned.1.call-done.payload_ref = bf16[512,3200]{1,0:T(8,128)(2,1)} async-done(((bf16[64,3200]{1,0:T(8,128)(2,1)}), bf16[512,3200]{1,0:T(8,128)(2,1)}) %all-gather.6.cloned.1.call-update) | async-done | bytes 3276816 | tf_op jit(solution)/shard_map/all_gather | solution.py:280
  74.9 44.7 %shard_map.140 = bf16[64,2048]{1,0:T(8,128)(2,1)} custom-call(s32[64]{0:T(128)} %lengths_ref.1, bf16[512,3200]{1,0:T(8,128)(2,1)} %all-gather.6.cloned.1.call-done.payload_ref, bf16[512,2048]{1,0:T(8,128)(2,1)} %key_up_ref.3, bf16[512,2048]{1,0:T(8,128)(2,1)} %value_up_ref.3, bf16[64,256,512]{2,1,0:T(8,128)(2,1)} %cache_ref.1, bf16[64,64,256]{2,1,0:T(8,128)(2,1)} %rope_ref.1), custom_call_target="tpu_custom_call" | custom-call | flops 4865392640 | bytes 20054016 | tf_op jit(solution)/shard_map/pallas_call | solution.py:110
  119.6 0.0 all-gather.8.cloned.1.call-update
  119.7 0.0 all-gather.4.cloned.1.call-done.query_latents_ref.latents_ref.extras_ref
  119.7 1.0 slice_convert_fusion
  120.7 0.2 fusion.1
  121.0 1.0 fusion.2
  122.0 1.0 pad_maximum_fusion.1.cosines_ref
  123.0 1.0 pad_maximum_fusion.2.sines_ref
  123.9 33.4 %shard_map.141 = bf16[512,2048]{1,0:T(8,128)(2,1)} custom-call(bf16[512,2176]{1,0:T(8,128)(2,1)} %all-gather.4.cloned.1.call-done.query_latents_ref.latents_ref.extras_ref, bf16[512,2176]{1,0:T(8,128)(2,1)} %all-gather.4.cloned.1.call-done.query_latents_ref.latents_ref.extras_ref, ...), custom_call_target="tpu_custom_call" | custom-call | flops 10200547328 | bytes 13631488 | tf_op jit(solution)/shard_map/pallas_call | solution.py:215
  157.3 10.4 %all-gather.8.cloned.1.call-done = bf16[512,2048]{1,0:T(8,128)(2,1)} async-done(((bf16[64,2048]{1,0:T(8,128)(2,1)}), bf16[512,2048]{1,0:T(8,128)(2,1)}) %all-gather.8.cloned.1.call-update) | async-done | bytes 2097168 | tf_op jit(solution)/shard_map/all_gather | solution.py:300
  167.8 2.8 %convolution_convert_fusion = bf16[64,2048]{1,0:T(8,128)(2,1)} fusion(bf16[512,2048]{1,0:T(8,128)(2,1)} %all-gather.8.cloned.1.call-done, s32[64]{0:T(128)S(1)} %multiply_add_fusion), kind=kOutput, calls=%fused_computation | convolution fusion | flops 134381568 | bytes 2359552 | tf_op jit(solution)/shard_map/dot_general | solution.py:313
  (7 shorter events, 0.0 us)
Async XLA Ops:
  7.2 67.7 %all-gather.6.cloned.1.call-start = ((), (), s32[]{:S(2)}) async-start(), calls=%async_computation.1 | async-start | bytes 3686400 | tf_op jit(solution)/shard_map/all_gather | solution.py:280
  9.8 109.9 %all-gather.4.cloned.1.call-start = ((), (), s32[]{:S(2)}) async-start(), calls=%async_computation | async-start | bytes 2785280 | tf_op jit(solution)/shard_map/all_gather | solution.py:290
  13.3 106.3 %copy-start = (s32[64]{0:T(128)S(1)}, s32[64]{0:T(128)}, u32[]{:S(2)}) copy-start(s32[64]{0:T(128)} %param.22) | copy-start | bytes 772
  13.3 106.3 %copy-start.1 = (s32[64]{0:T(128)S(1)}, s32[64]{0:T(128)}, u32[]{:S(2)}) copy-start(s32[64]{0:T(128)} %param.21) | copy-start | bytes 772
  13.4 154.4 %all-gather.8.cloned.1.call-start = ((), (), s32[]{:S(2)}) async-start(), calls=%async_computation.2 | async-start | bytes 2359296 | tf_op jit(solution)/shard_map/all_gather | solution.py:300
Sparse Core Ops, SparseCore 0:
  10.2 64.6 all-gather.5
  77.0 21.9 all-gather.3
  119.8 47.9 all-gather.7

commit v2 on v1

v2 whole, which is shorter than its diff:
```python
import functools
import math

import jax
import jax.numpy as jnp
from jax import lax
from jax.experimental import pallas as pl
from jax.experimental.pallas import tpu as pltpu
from jax.sharding import PartitionSpec as P

D_C = 512
D_NOPE = 128
D_ROPE = 64
D_V = 128
D_Q = D_NOPE + D_ROPE
ROPE_BASE = 10000.0
SCALE = D_Q ** (-0.5)
EXP2_SCALE = SCALE * math.log2(math.e)
MASKED = -1e30
DIGIT = 256
NT = (((1,), (1,)), ((), ()))
TN = (((0,), (0,)), ((), ()))
VMEM_BYTES = 56 * 1024 * 1024


def mm(a, b, dims=(((1,), (0,)), ((), ()))):
    return lax.dot_general(a, b, dims, preferred_element_type=jnp.float32)


def softmax_weights(scores):
    shifted = scores - jnp.max(scores, axis=-1, keepdims=True)
    grown = jnp.exp2(shifted * EXP2_SCALE)
    total = jnp.sum(grown, axis=-1, keepdims=True)
    return (grown * (1.0 / total)).astype(jnp.bfloat16)


def send_kernel(peers, most, owner_ref, slot_ref, queries_ref, payload_ref, back_ref):
    rows, width = queries_ref.shape
    owner = owner_ref[...].astype(jnp.float32)
    slot = slot_ref[...].astype(jnp.float32)
    across = jnp.broadcast_to(owner, (rows, rows))
    down = across.T
    before = lax.broadcasted_iota(jnp.int32, (rows, rows), 0) < lax.broadcasted_iota(
        jnp.int32, (rows, rows), 1
    )
    rank = jnp.sum(jnp.where((across == down) & before, 1.0, 0.0), axis=0, keepdims=True)
    me = lax.axis_index("req").astype(jnp.float32)
    hops = me - owner
    hops = jnp.where(hops < 0, hops + peers, hops)
    back_ref[...] = (hops * most + rank).astype(jnp.int32)
    index = lax.broadcasted_iota(jnp.int32, (peers * most, rows), 0).astype(jnp.float32)
    placing = index == owner * most + rank
    payload_ref[:, :width] = mm(
        jnp.where(placing, 1.0, 0.0).astype(jnp.bfloat16), queries_ref[...]
    ).astype(jnp.bfloat16)
    code = jnp.sum(jnp.where(placing, slot + 1.0, 0.0), axis=1, keepdims=True)
    payload_ref[:, width:] = jnp.broadcast_to(code, (peers * most, 128)).astype(jnp.bfloat16)


def pack_queries(queries, owner, slot, peers, most):
    rows, width = queries.shape
    return pl.pallas_call(
        functools.partial(send_kernel, peers, most),
        out_shape=(
            jax.ShapeDtypeStruct((peers * most, width + 128), jnp.bfloat16),
            jax.ShapeDtypeStruct((1, rows), jnp.int32),
        ),
        compiler_params=pltpu.CompilerParams(vmem_limit_bytes=VMEM_BYTES),
    )(owner[None, :], slot[None, :], queries)


def collect_kernel(back_ref, *refs):
    block_refs, out_ref = refs[:-1], refs[-1]
    blocks = jnp.concatenate([ref[...].astype(jnp.float32) for ref in block_refs], axis=0)
    index = lax.broadcasted_iota(jnp.int32, (blocks.shape[0], back_ref.shape[1]), 0)
    wanted = jnp.where(index == back_ref[...], 1.0, 0.0).astype(jnp.bfloat16)
    out_ref[...] = mm(wanted, blocks.astype(jnp.bfloat16), TN).astype(jnp.bfloat16)


def collect(back, blocks):
    return pl.pallas_call(
        collect_kernel,
        out_shape=jax.ShapeDtypeStruct((back.shape[1], blocks[0].shape[1]), jnp.bfloat16),
        compiler_params=pltpu.CompilerParams(vmem_limit_bytes=VMEM_BYTES),
    )(back, *blocks)


def decode_kernel(
    slots_per_step,
    head_count,
    peers,
    lengths_ref,
    payload_ref,
    key_up_ref,
    value_up_ref,
    cache_ref,
    rope_ref,
    *refs,
):
    out_refs, (query_ref, rope_query_ref, latent_out_ref) = refs[:peers], refs[peers:]
    step = pl.program_id(0)
    width = head_count * D_Q
    slot_count = query_ref.shape[1] // head_count
    chunks = query_ref.shape[0]
    rows = slots_per_step * head_count
    items = payload_ref.shape[0]

    def chosen():
        code = payload_ref[:, width : width + 1].astype(jnp.float32)
        slots = lax.broadcasted_iota(jnp.int32, (items, slot_count), 1).astype(jnp.float32)
        return jnp.where(code == slots + 1.0, 1.0, 0.0).astype(jnp.bfloat16)

    @pl.when(step == 0)
    def _():
        queries = mm(chosen(), payload_ref[:, :width], TN)
        for head in range(head_count):
            nope = queries[:, head * D_Q : head * D_Q + D_NOPE].astype(jnp.bfloat16)
            latent = mm(nope, key_up_ref[:, head * D_NOPE : (head + 1) * D_NOPE], NT)
            place = pl.ds(head, slot_count, stride=head_count)
            latent = latent.astype(jnp.bfloat16).astype(jnp.float32)
            for chunk in range(chunks):
                query_ref[chunk, place, :] = latent[:, chunk * 128 : (chunk + 1) * 128]
            rope = queries[:, head * D_Q + D_NOPE : (head + 1) * D_Q]
            rope_query_ref[place, :] = jnp.concatenate([rope, rope], axis=1)

    first = pl.multiple_of(step * slots_per_step, slots_per_step)
    here = pl.ds(pl.multiple_of(step * rows, rows), rows)
    columns = jnp.concatenate(
        [query_ref[chunk, here, :].T for chunk in range(chunks)], axis=0
    ).astype(jnp.bfloat16)
    rope_query = rope_query_ref[here, :D_ROPE].astype(jnp.bfloat16)
    owner = lax.broadcasted_iota(jnp.int32, columns.shape, 1) // head_count
    none = jnp.zeros_like(columns)
    turned = None
    for item in range(slots_per_step):
        part = mm(cache_ref[item], jnp.where(owner == item, columns, none))
        turned = part if turned is None else turned + part
    scores = turned.T
    lanes = lax.broadcasted_iota(jnp.int32, (head_count, cache_ref.shape[1]), 1)
    parts = []
    for item in range(slots_per_step):
        place = slice(item * head_count, (item + 1) * head_count)
        part = scores[place] + mm(rope_query[place], rope_ref[item])
        parts.append(jnp.where(lanes < lengths_ref[first + item], part, MASKED))
    weights = softmax_weights(jnp.concatenate(parts, axis=0))
    for item in range(slots_per_step):
        place = slice(item * head_count, (item + 1) * head_count)
        latent = mm(weights[place], cache_ref[item]).astype(jnp.bfloat16).astype(jnp.float32)
        below = pl.ds(pl.multiple_of(step * rows, rows) + item * head_count, head_count)
        for chunk in range(chunks):
            latent_out_ref[chunk, below, :] = latent[:, chunk * 128 : (chunk + 1) * 128]

    @pl.when(step == pl.num_programs(0) - 1)
    def _():
        me = lax.axis_index("req")
        most = items // peers
        source = lax.broadcasted_iota(jnp.int32, (items, items), 0) + me * most
        source = jnp.where(source >= items, source - items, source)
        order = source == lax.broadcasted_iota(jnp.int32, (items, items), 1)
        sending = mm(jnp.where(order, 1.0, 0.0).astype(jnp.bfloat16), chosen())
        sending = sending.astype(jnp.bfloat16)
        for head in range(head_count):
            strided = pl.ds(head, slot_count, stride=head_count)
            latent = jnp.concatenate(
                [latent_out_ref[chunk, strided, :] for chunk in range(chunks)], axis=1
            )
            place = slice(head * D_V, (head + 1) * D_V)
            answer = mm(latent.astype(jnp.bfloat16), value_up_ref[:, place])
            answer = mm(sending, answer.astype(jnp.bfloat16)).astype(jnp.bfloat16)
            for peer in range(peers):
                out_refs[peer][:, place] = answer[peer * most : (peer + 1) * most]


def decode_attention(payload, key_up, value_up, cache, rope_cache, lengths, peers):
    slot_count, cache_rows, _ = cache.shape
    head_count = key_up.shape[1] // D_NOPE
    per_step = 8
    most = payload.shape[0] // peers
    whole = lambda step, *_: (0, 0)
    flops = 2 * slot_count * head_count * (2 * D_NOPE * D_C + 17 * cache_rows * D_C)
    block = jax.ShapeDtypeStruct((most, head_count * D_V), jnp.bfloat16)
    return pl.pallas_call(
        functools.partial(decode_kernel, per_step, head_count, peers),
        out_shape=(block,) * peers,
        grid_spec=pltpu.PrefetchScalarGridSpec(
            num_scalar_prefetch=1,
            grid=(slot_count // per_step,),
            in_specs=[
                pl.BlockSpec(payload.shape, whole),
                pl.BlockSpec(key_up.shape, whole),
                pl.BlockSpec(value_up.shape, whole),
                pl.BlockSpec((per_step, cache_rows, D_C), lambda step, *_: (step, 0, 0)),
                pl.BlockSpec((per_step, D_ROPE, cache_rows), lambda step, *_: (step, 0, 0)),
            ],
            out_specs=(pl.BlockSpec(block.shape, whole),) * peers,
            scratch_shapes=[
                pltpu.VMEM((D_C // 128, slot_count * head_count, 128), jnp.float32),
                pltpu.VMEM((slot_count * head_count, 2 * D_ROPE), jnp.float32),
                pltpu.VMEM((D_C // 128, slot_count * head_count, 128), jnp.float32),
            ],
        ),
        compiler_params=pltpu.CompilerParams(vmem_limit_bytes=VMEM_BYTES),
        cost_estimate=pl.CostEstimate(
            flops=flops, bytes_accessed=cache.size * 2 + payload.size * 2, transcendentals=0
        ),
    )(lengths, payload, key_up, value_up, cache, rope_cache)


def prefill_kernel(
    heads,
    query_latents_ref,
    latents_ref,
    extras_ref,
    frequency_ref,
    query_up_ref,
    key_up_ref,
    value_up_ref,
    out_ref,
    bias_ref,
    cosine_ref,
    sine_ref,
    key_rope_ref,
):
    tokens = query_latents_ref.shape[0]
    lanes = lax.broadcasted_iota(jnp.int32, (tokens, D_NOPE), 1)
    low = lanes < D_ROPE
    leading = lanes % D_ROPE < D_ROPE // 2

    def rotated(values):
        swapped = jnp.where(
            leading,
            pltpu.roll(values, D_NOPE - D_ROPE // 2, 1),
            pltpu.roll(values, D_ROPE // 2, 1),
        )
        return values * cosine_ref[...] + swapped * sine_ref[...]

    @pl.when(pl.program_id(0) == 0)
    def _():
        extras = extras_ref[...].astype(jnp.float32)
        position = extras[:, D_ROPE : D_ROPE + 1] * DIGIT + extras[:, D_ROPE + 1 : D_ROPE + 2]
        row = lax.broadcasted_iota(jnp.int32, (tokens, tokens), 0).astype(jnp.float32)
        column = lax.broadcasted_iota(jnp.int32, (tokens, tokens), 1).astype(jnp.float32)
        visible = (column <= row) & (column >= row - position)
        bias_ref[...] = jnp.where(visible, 0.0, MASKED)
        angles = position * frequency_ref[...]
        cosine_ref[...] = jnp.cos(angles)
        sines = jnp.sin(angles)
        sine_ref[...] = jnp.where(leading, -sines, sines)
        twice = jnp.where(low, extras, pltpu.roll(extras, D_ROPE, 1))
        key_rope_ref[...] = rotated(twice).T[:D_ROPE].astype(jnp.bfloat16)

    projected = mm(query_latents_ref[...], query_up_ref[...])
    keys = mm(latents_ref[...], key_up_ref[...]).astype(jnp.bfloat16).T
    values = mm(latents_ref[...], value_up_ref[...]).astype(jnp.bfloat16)
    key_rope = key_rope_ref[...]
    none = jnp.zeros((D_ROPE, tokens), jnp.bfloat16)
    tile = 128
    for pair in range(heads // 2):
        base = pair * 2 * D_Q
        left = projected[:, base : base + D_NOPE].astype(jnp.bfloat16)
        middle = projected[:, base + D_NOPE : base + 2 * D_NOPE]
        middle = jnp.where(low, rotated(middle), middle).astype(jnp.bfloat16)
        right = projected[:, base + 2 * D_NOPE : base + 3 * D_NOPE]
        right = jnp.where(low, right, rotated(right)).astype(jnp.bfloat16)
        even = keys[2 * pair * D_NOPE : (2 * pair + 1) * D_NOPE]
        odd = keys[(2 * pair + 1) * D_NOPE : (2 * pair + 2) * D_NOPE]
        both = (
            (
                jnp.concatenate([left, middle], axis=1),
                jnp.concatenate([even, key_rope, none], axis=0),
            ),
            (
                jnp.concatenate([middle, right], axis=1),
                jnp.concatenate([none, odd, key_rope], axis=0),
            ),
        )
        for side, (query, key) in enumerate(both):
            place = slice((2 * pair + side) * D_V, (2 * pair + side + 1) * D_V)
            value = values[:, place]
            for begin in range(0, tokens, tile):
                end = begin + tile
                scores = mm(query[begin:end], key[:, :end]) + bias_ref[begin:end, :end]
                weights = softmax_weights(scores)
                out_ref[begin:end, place] = mm(weights, value[:end]).astype(jnp.bfloat16)


def prefill_attention(gathered, query_up, key_up, value_up):
    tokens = gathered.shape[0]
    latent_width = query_up.shape[0]
    head_count = key_up.shape[1] // D_NOPE
    extra_block = (latent_width + D_C) // D_NOPE
    heads = 4
    half_width = D_ROPE // 2
    frequency = ROPE_BASE ** (-jnp.arange(half_width, dtype=jnp.float32) / half_width)
    whole = lambda step: (0, 0)
    across = lambda step: (0, step)
    flops = 2 * tokens * head_count * (latent_width * D_Q + 2 * D_C * D_NOPE + tokens * 384)
    return pl.pallas_call(
        functools.partial(prefill_kernel, heads),
        out_shape=jax.ShapeDtypeStruct((tokens, head_count * D_V), jnp.bfloat16),
        grid=(head_count // heads,),
        in_specs=[
            pl.BlockSpec((tokens, latent_width), whole),
            pl.BlockSpec((tokens, D_C), lambda step: (0, latent_width // D_C)),
            pl.BlockSpec((tokens, D_NOPE), lambda step: (0, extra_block)),
            pl.BlockSpec((1, D_NOPE), whole),
            pl.BlockSpec((latent_width, heads * D_Q), across),
            pl.BlockSpec((D_C, heads * D_NOPE), across),
            pl.BlockSpec((D_C, heads * D_V), across),
        ],
        out_specs=pl.BlockSpec((tokens, heads * D_V), across),
        scratch_shapes=[
            pltpu.VMEM((tokens, tokens), jnp.float32),
            pltpu.VMEM((tokens, D_NOPE), jnp.float32),
            pltpu.VMEM((tokens, D_NOPE), jnp.float32),
            pltpu.VMEM((D_ROPE, tokens), jnp.bfloat16),
        ],
        compiler_params=pltpu.CompilerParams(vmem_limit_bytes=VMEM_BYTES),
        cost_estimate=pl.CostEstimate(
            flops=flops, bytes_accessed=query_up.size * 2 + key_up.size * 4, transcendentals=0
        ),
    )(
        gathered,
        gathered,
        gathered,
        jnp.tile(frequency, 4)[None, :],
        query_up,
        key_up,
        value_up,
    )


def on_device(
    prompt_query_latents,
    prompt_latents,
    prompt_rotary_keys,
    positions,
    query_up_weight,
    key_up_weight,
    value_up_weight,
    decode_queries,
    decode_owner_index,
    decode_cache_slot,
    latent_cache_rows,
    rotated_cache_keys,
    cache_live_lengths,
):
    row_count = decode_queries.shape[0]
    token_count = prompt_latents.shape[0]
    peers = lax.axis_size("req")
    most = max(2, row_count * 2 // peers)

    lane = lax.broadcasted_iota(jnp.int32, (token_count, D_ROPE), 1)
    place = positions[:, None]
    digits = jnp.where(lane == 0, place // DIGIT, jnp.where(lane == 1, place % DIGIT, 0))
    prompt = jnp.concatenate(
        [
            prompt_query_latents,
            prompt_latents,
            prompt_rotary_keys.T,
            digits.astype(jnp.bfloat16),
        ],
        axis=1,
    )
    prompt = lax.all_gather(prompt, "head", axis=0, tiled=True)

    payload, back = pack_queries(
        decode_queries, decode_owner_index, decode_cache_slot, peers, most
    )
    payload = lax.all_to_all(
        payload.reshape(peers, most, -1), "req", split_axis=0, concat_axis=0, tiled=True
    ).reshape(peers * most, -1)
    answers = decode_attention(
        payload,
        key_up_weight,
        value_up_weight,
        latent_cache_rows,
        rotated_cache_keys,
        cache_live_lengths,
        peers,
    )
    returned = [answers[0]] + [
        lax.ppermute(answers[hop], "req", [(i, (i + hop) % peers) for i in range(peers)])
        for hop in range(1, peers)
    ]
    prompt, _ = lax.optimization_barrier((prompt, answers[0]))
    prompt_attention_output = prefill_attention(
        prompt, query_up_weight, key_up_weight, value_up_weight
    )
    back, prompt_attention_output = lax.optimization_barrier((back, prompt_attention_output))
    return (prompt_attention_output, collect(back, returned))


def solution(mesh):
    placed = (
        P(("req", "head"), None),
        P(("req", "head"), None),
        P(None, ("req", "head")),
        P(("req", "head")),
        P(None, "head"),
        P(None, "head"),
        P(None, "head"),
        P("req", "head"),
        P("req"),
        P("req"),
        P("req", None, None),
        P("req", None, None),
        P("req"),
    )
    return jax.shard_map(
        on_device,
        mesh=mesh,
        in_specs=placed,
        out_specs=(P("req", "head"), P("req", "head")),
        check_vma=False,
    )
```

time: 177 us -> 119 us (0.67)
  waiting for transfers between devices: 72 us -> 0.1 us
  blocking collectives: 0 us -> 29 us
  Pallas kernels: 78.2 us -> 59.3 us
  starting transfers between devices: 0.12 us -> 10.3 us
  other arithmetic: 7.51 us -> 0.79 us
  matrix products: 2.81 us -> 0 us
  local copies, waits for them, and re-layouts: 2.7 us -> 4.6 us
    all_gather x2 -> x0, waiting for transfers between devices: 71.9 us -> none  [the longest x1 61.5 us: on_device(): payload = lax.all_gather(payload, 'req', axis=0, tiled=True)]
    all_to_all x0 -> x1, blocking collectives: none -> 29 us  [on_device(): lax.all_to_all(payload.reshape(peers, most, -1), 'req', split_axis=0, con...]
    pallas_call x2 -> x4, Pallas kernels: 78.2 us -> 59.3 us  [the longest x1 33.7 us: prefill_attention(): pl.pallas_call(functools.partial(prefill_kernel, heads), out_shape=jax.Sh...]
    ppermute x0 -> x7, starting transfers between devices: none -> 10.2 us  [on_device(): lax.ppermute(answers[hop], 'req', [(i, (i + hop) % peers) for i in range(...]
    concatenate x3 -> x0, other arithmetic: 3.72 us -> none  [the longest x1 1.78 us: on_device(): jnp.concatenate([decode_queries, digits(decode_owner_index, decode_cache_...]
    dot_general x1 -> x0, matrix products: 2.81 us -> none  [on_device(): jnp.dot(wanted, returned, preferred_element_type=jnp.float32)]
    convert_element_type x4 -> x1, other arithmetic: 2.1 us -> 0.11 us  [on_device(): digits.astype(jnp.bfloat16)]
  transfers between devices with their start and end apart: 3 -> 8, of which waited for: 2 -> 1; matrix products, arithmetic and copies ran while one was open for 4% -> 1% of each run, Pallas kernels for 44% -> 48%
where the time goes in v2:
time: 119 us; the launch traced here: 118 us
  Pallas kernels  59.3 us (50%)
  blocking collectives  29 us (24%)
  between operations  14.1 us (12%)
  starting transfers between devices  10.3 us (9%)
  local copies, waits for them, and re-layouts  4.6 us (4%)
    pallas_call x1, Pallas kernels, prefill_attention(): pl.pallas_call(functools.partial(prefill_kernel, heads), out_shape=jax.Sh...  33.7 us
    all_to_all x1, blocking collectives, on_device(): lax.all_to_all(payload.reshape(peers, most, -1), 'req', split_axis=0, con...  29 us
    pallas_call x1, Pallas kernels, decode_attention(): pl.pallas_call(functools.partial(decode_kernel, per_step, head_count, pee...  21.2 us
    ppermute x7, starting transfers between devices, on_device(): lax.ppermute(answers[hop], 'req', [(i, (i + hop) % peers) for i in range(...  10.2 us
  transfers between devices with their start and end apart: 8, of which 1 were waited for; matrix products, arithmetic and copies ran while one was open for 1% of the time, Pallas kernels for 48%

profile of v2, /device:TPU:0, one launch (start us, length us, event | category | flops | bytes accessed | tf_op | source)
XLA Modules:
  0.0 118.2 jit_solution(1697892655848021544)
XLA Ops:
  7.2 0.0 all-gather.2.cloned.1.call-start
  7.2 0.7 and_select_fusion.1
  7.9 0.8 copy.15
  8.7 0.1 select_convert_fusion
  8.8 1.8 %concatenate.3 = bf16[128,2176]{1,0:T(8,128)(2,1)} concatenate(bf16[128,1536]{1,0:T(8,128)(2,1)} %param.13, bf16[128,512]{1,0:T(8,128)(2,1)} %param.14, bf16[128,64]{1,0:T(8,128)(2,1)S(1)} %bitcast.7, bf16[128,64]{1,0:T(8,128)(2,1)S(1)} %select_convert_fusion), dimensions={1} | concatenate | bytes 1114112 | tf_op jit(solution)/shard_map/concatenate | solution.py:356
  10.7 0.0 all-gather.2.cloned.1.call-update
  10.7 2.4 %shard_map.140 = (bf16[128,3200]{1,0:T(8,128)(2,1)}, s32[1,64]{1,0:T(1,128)}) custom-call(s32[1,64]{1,0:T(1,128)} %bitcast.8, s32[1,64]{1,0:T(1,128)} %bitcast.9, bf16[64,3072]{1,0:T(8,128)(2,1)} %queries_ref.1), custom_call_target="tpu_custom_call" | custom-call | tf_op jit(solution)/shard_map/pallas_call | solution.py:62
  13.1 29.0 %all_to_all.5 = bf16[8,16,3200]{2,1,0:T(8,128)(2,1)} all-to-all(bf16[8,16,3200]{2,1,0:T(8,128)(2,1)} %bitcast.6), channel_id=1, replica_groups=mesh['req'=8,'head'=4] {'req'}, dimensions={0} | all-to-all | bytes 1638400 | tf_op jit(solution)/shard_map/all_to_all | solution.py:370
  42.0 21.2 %shard_map.141 = (bf16[16,2048]{1,0:T(8,128)(2,1)}, bf16[16,2048]{1,0:T(8,128)(2,1)}, bf16[16,2048]{1,0:T(8,128)(2,1)}, bf16[16,2048]{1,0:T(8,128)(2,1)}, bf16[1...) custom-call(s32[64]{0:T(128)} %lengths_ref.1, ...), custom_call_target="tpu_custom_call" | custom-call | flops 4831838208 | bytes 17596416 | tf_op jit(solution)/shard_map/pallas_call | solution.py:182
  63.3 0.7 collective-permute-start
  64.0 0.5 collective-permute-start.1
  64.5 0.7 broadcast_in_dim_tile.3.frequency_ref
  65.2 2.3 %collective-permute-start.2 = (bf16[16,2048]{1,0:T(8,128)(2,1)}, bf16[16,2048]{1,0:T(8,128)(2,1)S(1)}, u32[]{:S(2)}, u32[]{:S(2)}) collective-permute-start(bf16[16,2048]{1,0:T(8,128)(2,1)} %get-tuple-element.23), channel_id=1, source_target_pairs={{0,12},{4,16},{8,20},{12,24},{16,28},{20,0},{24,4},{28,8},{1,13},{... | collective-permute-start | bytes 196616 | tf_op jit(solution)/shard_map/ppermute | solution.py:383
  67.4 2.5 %collective-permute-start.3 = (bf16[16,2048]{1,0:T(8,128)(2,1)}, bf16[16,2048]{1,0:T(8,128)(2,1)S(1)}, u32[]{:S(2)}, u32[]{:S(2)}) collective-permute-start(bf16[16,2048]{1,0:T(8,128)(2,1)} %get-tuple-element.24), channel_id=1, source_target_pairs={{0,16},{4,20},{8,24},{12,28},{16,0},{20,4},{24,8},{28,12},{1,17},{... | collective-permute-start | bytes 196616 | tf_op jit(solution)/shard_map/ppermute | solution.py:383
  69.9 0.6 collective-permute-start.4
  70.5 0.1 collective-permute-done.refs_1_
  70.6 1.8 %collective-permute-start.5 = (bf16[16,2048]{1,0:T(8,128)(2,1)}, bf16[16,2048]{1,0:T(8,128)(2,1)S(1)}, u32[]{:S(2)}, u32[]{:S(2)}) collective-permute-start(bf16[16,2048]{1,0:T(8,128)(2,1)} %get-tuple-element.26), channel_id=1, source_target_pairs={{0,24},{4,28},{8,0},{12,4},{16,8},{20,12},{24,16},{28,20},{1,25},{... | collective-permute-start | bytes 196616 | tf_op jit(solution)/shard_map/ppermute | solution.py:383
  72.4 1.9 %collective-permute-start.6 = (bf16[16,2048]{1,0:T(8,128)(2,1)}, bf16[16,2048]{1,0:T(8,128)(2,1)S(1)}, u32[]{:S(2)}, u32[]{:S(2)}) collective-permute-start(bf16[16,2048]{1,0:T(8,128)(2,1)} %get-tuple-element.27), channel_id=1, source_target_pairs={{0,28},{4,0},{8,4},{12,8},{16,12},{20,16},{24,20},{28,24},{1,29},{... | collective-permute-start | bytes 196616 | tf_op jit(solution)/shard_map/ppermute | solution.py:383
  74.3 33.7 %shard_map.142 = bf16[512,2048]{1,0:T(8,128)(2,1)} custom-call(bf16[512,2176]{1,0:T(8,128)(2,1)} %all-gather.2.cloned.1.call-done.query_latents_ref.latents_ref.extras_ref, bf16[512,2176]{1,0:T(8,128)(2,1)} %all-gather.2.cloned.1.call-done.query_latents_ref.latents_ref.extras_ref, ...), custom_call_target="tpu_custom_call" | custom-call | flops 10200547328 | bytes 13631488 | tf_op jit(solution)/shard_map/pallas_call | solution.py:298
  108.1 0.5 copy-done.2
  108.6 0.0 copy-done.3
  108.7 0.0 copy-done.4
  108.7 0.6 copy-done.6
  109.3 2.0 %shard_map.143 = bf16[64,2048]{1,0:T(8,128)(2,1)} custom-call(s32[1,64]{1,0:T(1,128)} %get-tuple-element.20.back_ref, bf16[16,2048]{1,0:T(8,128)(2,1)} %get-tuple-element.17.refs_0_, bf16[16,2048]{1,0:T(8,128)(2,1)} %copy-done, bf16[16,2048]{1,0:T(8,128)(2,1)} %copy-done.1, bf16[16,2048]{1,0:T(8,128)(2,1)} %copy-done.2, bf16[16,2048]{1,0:T(8,128)(2,1)} %copy-done.3, ...), custom_call_target="tpu_custom_call" | custom-call | tf_op jit(solution)/shard_map/pallas_call | solution.py:81
  (20 shorter events, 0.1 us)
Async XLA Ops:
  7.2 63.3 %all-gather.2.cloned.1.call-start = ((), (), s32[]{:S(2)}) async-start(), calls=%async_computation.1 | async-start | bytes 2785280 | tf_op jit(solution)/shard_map/all_gather | solution.py:365
  63.3 7.3 %collective-permute-start = (bf16[16,2048]{1,0:T(8,128)(2,1)}, bf16[16,2048]{1,0:T(8,128)(2,1)S(1)}, u32[]{:S(2)}, u32[]{:S(2)}) collective-permute-start(bf16[16,2048]{1,0:T(8,128)(2,1)} %get-tuple-element.21), channel_id=1, source_target_pairs={{0,4},{4,8},{8,12},{12,16},{16,20},{20,24},{24,28},{28,0},{1,5},{5... | collective-permute-start | bytes 196616 | tf_op jit(solution)/shard_map/ppermute | solution.py:383
  64.0 8.4 %collective-permute-start.1 = (bf16[16,2048]{1,0:T(8,128)(2,1)}, bf16[16,2048]{1,0:T(8,128)(2,1)S(1)}, u32[]{:S(2)}, u32[]{:S(2)}) collective-permute-start(bf16[16,2048]{1,0:T(8,128)(2,1)} %get-tuple-element.22), channel_id=1, source_target_pairs={{0,8},{4,12},{8,16},{12,20},{16,24},{20,28},{24,0},{28,4},{1,9},{5... | collective-permute-start | bytes 196616 | tf_op jit(solution)/shard_map/ppermute | solution.py:383
  65.2 42.8 %collective-permute-start.2 = (bf16[16,2048]{1,0:T(8,128)(2,1)}, bf16[16,2048]{1,0:T(8,128)(2,1)S(1)}, u32[]{:S(2)}, u32[]{:S(2)}) collective-permute-start(bf16[16,2048]{1,0:T(8,128)(2,1)} %get-tuple-element.23), channel_id=1, source_target_pairs={{0,12},{4,16},{8,20},{12,24},{16,28},{20,0},{24,4},{28,8},{1,13},{... | collective-permute-start | bytes 196616 | tf_op jit(solution)/shard_map/ppermute | solution.py:383
  67.4 40.6 %collective-permute-start.3 = (bf16[16,2048]{1,0:T(8,128)(2,1)}, bf16[16,2048]{1,0:T(8,128)(2,1)S(1)}, u32[]{:S(2)}, u32[]{:S(2)}) collective-permute-start(bf16[16,2048]{1,0:T(8,128)(2,1)} %get-tuple-element.24), channel_id=1, source_target_pairs={{0,16},{4,20},{8,24},{12,28},{16,0},{20,4},{24,8},{28,12},{1,17},{... | collective-permute-start | bytes 196616 | tf_op jit(solution)/shard_map/ppermute | solution.py:383
  69.9 38.1 %collective-permute-start.4 = (bf16[16,2048]{1,0:T(8,128)(2,1)}, bf16[16,2048]{1,0:T(8,128)(2,1)S(1)}, u32[]{:S(2)}, u32[]{:S(2)}) collective-permute-start(bf16[16,2048]{1,0:T(8,128)(2,1)} %get-tuple-element.25), channel_id=1, source_target_pairs={{0,20},{4,24},{8,28},{12,0},{16,4},{20,8},{24,12},{28,16},{1,21},{... | collective-permute-start | bytes 196616 | tf_op jit(solution)/shard_map/ppermute | solution.py:383
  70.6 37.4 %copy-start = (bf16[16,2048]{1,0:T(8,128)(2,1)}, bf16[16,2048]{1,0:T(8,128)(2,1)S(1)}, u32[]{:S(2)}) copy-start(bf16[16,2048]{1,0:T(8,128)(2,1)S(1)} %collective-permute-done.refs_1_) | copy-start | bytes 196612
  70.6 37.5 %collective-permute-start.5 = (bf16[16,2048]{1,0:T(8,128)(2,1)}, bf16[16,2048]{1,0:T(8,128)(2,1)S(1)}, u32[]{:S(2)}, u32[]{:S(2)}) collective-permute-start(bf16[16,2048]{1,0:T(8,128)(2,1)} %get-tuple-element.26), channel_id=1, source_target_pairs={{0,24},{4,28},{8,0},{12,4},{16,8},{20,12},{24,16},{28,20},{1,25},{... | collective-permute-start | bytes 196616 | tf_op jit(solution)/shard_map/ppermute | solution.py:383
  72.4 35.6 %copy-start.1 = (bf16[16,2048]{1,0:T(8,128)(2,1)}, bf16[16,2048]{1,0:T(8,128)(2,1)S(1)}, u32[]{:S(2)}) copy-start(bf16[16,2048]{1,0:T(8,128)(2,1)S(1)} %collective-permute-done.1.refs_2_) | copy-start | bytes 196612
  72.4 35.7 %collective-permute-start.6 = (bf16[16,2048]{1,0:T(8,128)(2,1)}, bf16[16,2048]{1,0:T(8,128)(2,1)S(1)}, u32[]{:S(2)}, u32[]{:S(2)}) collective-permute-start(bf16[16,2048]{1,0:T(8,128)(2,1)} %get-tuple-element.27), channel_id=1, source_target_pairs={{0,28},{4,0},{8,4},{12,8},{16,12},{20,16},{24,20},{28,24},{1,29},{... | collective-permute-start | bytes 196616 | tf_op jit(solution)/shard_map/ppermute | solution.py:383
  108.0 0.6 copy-start.2
  108.0 0.6 copy-start.3
  108.0 0.6 copy-start.4
  108.1 0.6 copy-start.5
  108.7 0.6 copy-start.6
Sparse Core Ops, SparseCore 0:
  10.8 26.0 all-gather.1

commit v3 on v2

--- a/solution.py
+++ b/solution.py
@@ -34,7 +34,41 @@
     return (grown * (1.0 / total)).astype(jnp.bfloat16)
 
 
-def send_kernel(peers, most, owner_ref, slot_ref, queries_ref, payload_ref, back_ref):
+def exchange(peers, source_ref, target_ref, local_sem, send_sem, recv_sem):
+    me = lax.axis_index("req")
+    barrier = pltpu.get_barrier_semaphore()
+    for hop in range(1, peers):
+        pl.semaphore_signal(
+            barrier,
+            inc=1,
+            device_id={"req": lax.rem(me + hop, peers)},
+            device_id_type=pl.DeviceIdType.MESH,
+        )
+    pl.semaphore_wait(barrier, peers - 1)
+    copies = []
+    for hop in range(1, peers):
+        target = lax.rem(me + hop, peers)
+        copy = pltpu.make_async_remote_copy(
+            src_ref=source_ref.at[target],
+            dst_ref=target_ref.at[me],
+            send_sem=send_sem.at[hop],
+            recv_sem=recv_sem.at[hop],
+            device_id={"req": target},
+            device_id_type=pl.DeviceIdType.MESH,
+        )
+        copy.start()
+        copies.append(copy)
+    own = pltpu.make_async_copy(source_ref.at[me], target_ref.at[me], local_sem)
+    own.start()
+    own.wait()
+    for copy in copies:
+        copy.wait()
+
+
+def send_kernel(
+    owner_ref, slot_ref, queries_ref, payload_ref, back_ref, packed_ref, local_sem, send_sem, recv_sem
+):
+    peers, most, _ = payload_ref.shape
     rows, width = queries_ref.shape
     owner = owner_ref[...].astype(jnp.float32)
     slot = slot_ref[...].astype(jnp.float32)
@@ -44,75 +78,101 @@
         jnp.int32, (rows, rows), 1
     )
     rank = jnp.sum(jnp.where((across == down) & before, 1.0, 0.0), axis=0, keepdims=True)
-    me = lax.axis_index("req").astype(jnp.float32)
-    hops = me - owner
-    hops = jnp.where(hops < 0, hops + peers, hops)
-    back_ref[...] = (hops * most + rank).astype(jnp.int32)
+    place = owner * most + rank
+    back_ref[...] = place.astype(jnp.int32)
     index = lax.broadcasted_iota(jnp.int32, (peers * most, rows), 0).astype(jnp.float32)
-    placing = index == owner * most + rank
-    payload_ref[:, :width] = mm(
-        jnp.where(placing, 1.0, 0.0).astype(jnp.bfloat16), queries_ref[...]
-    ).astype(jnp.bfloat16)
+    placing = index == place
+    packed = mm(jnp.where(placing, 1.0, 0.0).astype(jnp.bfloat16), queries_ref[...])
     code = jnp.sum(jnp.where(placing, slot + 1.0, 0.0), axis=1, keepdims=True)
-    payload_ref[:, width:] = jnp.broadcast_to(code, (peers * most, 128)).astype(jnp.bfloat16)
-
-
-def pack_queries(queries, owner, slot, peers, most):
+    packed_ref[:, :, :width] = packed.reshape(peers, most, width).astype(jnp.bfloat16)
+    packed_ref[:, :, width:] = (
+        jnp.broadcast_to(code, (peers * most, 128)).reshape(peers, most, 128).astype(jnp.bfloat16)
+    )
+    exchange(peers, packed_ref, payload_ref, local_sem, send_sem, recv_sem)
+
+
+def exchange_sems(peers):
+    return [
+        pltpu.SemaphoreType.DMA,
+        pltpu.SemaphoreType.DMA((peers,)),
+        pltpu.SemaphoreType.DMA((peers,)),
+    ]
+
+
+def send_queries(queries, owner, slot, peers, most):
     rows, width = queries.shape
+    vmem = pl.BlockSpec(memory_space=pltpu.VMEM)
     return pl.pallas_call(
-        functools.partial(send_kernel, peers, most),
+        send_kernel,
         out_shape=(
-            jax.ShapeDtypeStruct((peers * most, width + 128), jnp.bfloat16),
+            jax.ShapeDtypeStruct((peers, most, width + 128), jnp.bfloat16),
             jax.ShapeDtypeStruct((1, rows), jnp.int32),
         ),
-        compiler_params=pltpu.CompilerParams(vmem_limit_bytes=VMEM_BYTES),
+        in_specs=[vmem] * 3,
+        out_specs=(pl.BlockSpec(memory_space=pl.ANY), vmem),
+        scratch_shapes=[pltpu.VMEM((peers, most, width + 128), jnp.bfloat16)]
+        + exchange_sems(peers),
+        compiler_params=pltpu.CompilerParams(
+            vmem_limit_bytes=VMEM_BYTES, collective_id=0, has_side_effects=True
+        ),
     )(owner[None, :], slot[None, :], queries)
 
 
-def collect_kernel(back_ref, *refs):
-    block_refs, out_ref = refs[:-1], refs[-1]
-    blocks = jnp.concatenate([ref[...].astype(jnp.float32) for ref in block_refs], axis=0)
-    index = lax.broadcasted_iota(jnp.int32, (blocks.shape[0], back_ref.shape[1]), 0)
+def collect_kernel(back_ref, answers_ref, out_ref, landed_ref, local_sem, send_sem, recv_sem):
+    peers, most, width = landed_ref.shape
+    exchange(peers, answers_ref, landed_ref, local_sem, send_sem, recv_sem)
+    blocks = landed_ref[...].astype(jnp.float32).reshape(peers * most, width)
+    index = lax.broadcasted_iota(jnp.int32, (peers * most, back_ref.shape[1]), 0)
     wanted = jnp.where(index == back_ref[...], 1.0, 0.0).astype(jnp.bfloat16)
     out_ref[...] = mm(wanted, blocks.astype(jnp.bfloat16), TN).astype(jnp.bfloat16)
 
 
-def collect(back, blocks):
+def return_answers(back, answers):
+    peers = answers.shape[0]
+    vmem = pl.BlockSpec(memory_space=pltpu.VMEM)
     return pl.pallas_call(
         collect_kernel,
-        out_shape=jax.ShapeDtypeStruct((back.shape[1], blocks[0].shape[1]), jnp.bfloat16),
-        compiler_params=pltpu.CompilerParams(vmem_limit_bytes=VMEM_BYTES),
-    )(back, *blocks)
+        out_shape=jax.ShapeDtypeStruct((back.shape[1], answers.shape[2]), jnp.bfloat16),
+        in_specs=[vmem, pl.BlockSpec(memory_space=pl.ANY)],
+        out_specs=vmem,
+        scratch_shapes=[pltpu.VMEM(answers.shape, jnp.bfloat16)] + exchange_sems(peers),
+        compiler_params=pltpu.CompilerParams(
+            vmem_limit_bytes=VMEM_BYTES, collective_id=1, has_side_effects=True
+        ),
+    )(back, answers)
 
 
 def decode_kernel(
     slots_per_step,
     head_count,
-    peers,
     lengths_ref,
     payload_ref,
     key_up_ref,
     value_up_ref,
     cache_ref,
     rope_ref,
-    *refs,
+    out_ref,
+    query_ref,
+    rope_query_ref,
+    latent_out_ref,
 ):
-    out_refs, (query_ref, rope_query_ref, latent_out_ref) = refs[:peers], refs[peers:]
     step = pl.program_id(0)
     width = head_count * D_Q
     slot_count = query_ref.shape[1] // head_count
     chunks = query_ref.shape[0]
     rows = slots_per_step * head_count
-    items = payload_ref.shape[0]
+    peers, most, _ = payload_ref.shape
+    items = peers * most
 
     def chosen():
-        code = payload_ref[:, width : width + 1].astype(jnp.float32)
+        code = payload_ref[:, :, width:].astype(jnp.float32).reshape(items, 128)[:, :1]
         slots = lax.broadcasted_iota(jnp.int32, (items, slot_count), 1).astype(jnp.float32)
         return jnp.where(code == slots + 1.0, 1.0, 0.0).astype(jnp.bfloat16)
 
     @pl.when(step == 0)
     def _():
-        queries = mm(chosen(), payload_ref[:, :width], TN)
+        received = payload_ref[:, :, :width].reshape(items, width)
+        queries = mm(chosen(), received, TN)
         for head in range(head_count):
             nope = queries[:, head * D_Q : head * D_Q + D_NOPE].astype(jnp.bfloat16)
             latent = mm(nope, key_up_ref[:, head * D_NOPE : (head + 1) * D_NOPE], NT)
@@ -152,13 +212,7 @@
 
     @pl.when(step == pl.num_programs(0) - 1)
     def _():
-        me = lax.axis_index("req")
-        most = items // peers
-        source = lax.broadcasted_iota(jnp.int32, (items, items), 0) + me * most
-        source = jnp.where(source >= items, source - items, source)
-        order = source == lax.broadcasted_iota(jnp.int32, (items, items), 1)
-        sending = mm(jnp.where(order, 1.0, 0.0).astype(jnp.bfloat16), chosen())
-        sending = sending.astype(jnp.bfloat16)
+        sending = chosen()
         for head in range(head_count):
             strided = pl.ds(head, slot_count, stride=head_count)
             latent = jnp.concatenate(
@@ -167,32 +221,32 @@
             place = slice(head * D_V, (head + 1) * D_V)
             answer = mm(latent.astype(jnp.bfloat16), value_up_ref[:, place])
             answer = mm(sending, answer.astype(jnp.bfloat16)).astype(jnp.bfloat16)
-            for peer in range(peers):
-                out_refs[peer][:, place] = answer[peer * most : (peer + 1) * most]
-
-
-def decode_attention(payload, key_up, value_up, cache, rope_cache, lengths, peers):
+            out_ref[:, :, place] = answer.reshape(peers, most, D_V)
+
+
+def decode_attention(payload, key_up, value_up, cache, rope_cache, lengths):
     slot_count, cache_rows, _ = cache.shape
     head_count = key_up.shape[1] // D_NOPE
     per_step = 8
-    most = payload.shape[0] // peers
+    peers, most, _ = payload.shape
     whole = lambda step, *_: (0, 0)
+    single = lambda step, *_: (0, 0, 0)
     flops = 2 * slot_count * head_count * (2 * D_NOPE * D_C + 17 * cache_rows * D_C)
-    block = jax.ShapeDtypeStruct((most, head_count * D_V), jnp.bfloat16)
+    block = jax.ShapeDtypeStruct((peers, most, head_count * D_V), jnp.bfloat16)
     return pl.pallas_call(
-        functools.partial(decode_kernel, per_step, head_count, peers),
-        out_shape=(block,) * peers,
+        functools.partial(decode_kernel, per_step, head_count),
+        out_shape=block,
         grid_spec=pltpu.PrefetchScalarGridSpec(
             num_scalar_prefetch=1,
             grid=(slot_count // per_step,),
             in_specs=[
-                pl.BlockSpec(payload.shape, whole),
+                pl.BlockSpec(payload.shape, single),
                 pl.BlockSpec(key_up.shape, whole),
                 pl.BlockSpec(value_up.shape, whole),
                 pl.BlockSpec((per_step, cache_rows, D_C), lambda step, *_: (step, 0, 0)),
                 pl.BlockSpec((per_step, D_ROPE, cache_rows), lambda step, *_: (step, 0, 0)),
             ],
-            out_specs=(pl.BlockSpec(block.shape, whole),) * peers,
+            out_specs=pl.BlockSpec(block.shape, single),
             scratch_shapes=[
                 pltpu.VMEM((D_C // 128, slot_count * head_count, 128), jnp.float32),
                 pltpu.VMEM((slot_count * head_count, 2 * D_ROPE), jnp.float32),
@@ -254,7 +308,8 @@
     values = mm(latents_ref[...], value_up_ref[...]).astype(jnp.bfloat16)
     key_rope = key_rope_ref[...]
     none = jnp.zeros((D_ROPE, tokens), jnp.bfloat16)
-    tile = 128
+    tile = min(256, tokens)
+    work = []
     for pair in range(heads // 2):
         base = pair * 2 * D_Q
         left = projected[:, base : base + D_NOPE].astype(jnp.bfloat16)
@@ -276,12 +331,18 @@
         )
         for side, (query, key) in enumerate(both):
             place = slice((2 * pair + side) * D_V, (2 * pair + side + 1) * D_V)
-            value = values[:, place]
             for begin in range(0, tokens, tile):
-                end = begin + tile
-                scores = mm(query[begin:end], key[:, :end]) + bias_ref[begin:end, :end]
-                weights = softmax_weights(scores)
-                out_ref[begin:end, place] = mm(weights, value[:end]).astype(jnp.bfloat16)
+                work.append((query, key, place, begin, begin + tile))
+
+    def score(query, key, place, begin, end):
+        return mm(query[begin:end], key[:, :end]) + bias_ref[begin:end, :end]
+
+    scores = score(*work[0])
+    for index, (_, _, place, begin, end) in enumerate(work):
+        following = score(*work[index + 1]) if index + 1 < len(work) else None
+        weights = softmax_weights(scores)
+        out_ref[begin:end, place] = mm(weights, values[:end, place]).astype(jnp.bfloat16)
+        scores = following
 
 
 def prefill_attention(gathered, query_up, key_up, value_up):
@@ -364,12 +425,9 @@
     )
     prompt = lax.all_gather(prompt, "head", axis=0, tiled=True)
 
-    payload, back = pack_queries(
+    payload, back = send_queries(
         decode_queries, decode_owner_index, decode_cache_slot, peers, most
     )
-    payload = lax.all_to_all(
-        payload.reshape(peers, most, -1), "req", split_axis=0, concat_axis=0, tiled=True
-    ).reshape(peers * most, -1)
     answers = decode_attention(
         payload,
         key_up_weight,
@@ -377,18 +435,13 @@
         latent_cache_rows,
         rotated_cache_keys,
         cache_live_lengths,
-        peers,
-    )
-    returned = [answers[0]] + [
-        lax.ppermute(answers[hop], "req", [(i, (i + hop) % peers) for i in range(peers)])
-        for hop in range(1, peers)
-    ]
-    prompt, _ = lax.optimization_barrier((prompt, answers[0]))
+    )
+    decode_out = return_answers(back, answers)
+    prompt, _ = lax.optimization_barrier((prompt, answers))
     prompt_attention_output = prefill_attention(
         prompt, query_up_weight, key_up_weight, value_up_weight
     )
-    back, prompt_attention_output = lax.optimization_barrier((back, prompt_attention_output))
-    return (prompt_attention_output, collect(back, returned))
+    return (prompt_attention_output, decode_out)
 
 
 def solution(mesh):

time: 119 us -> 103 us (0.87)
  blocking collectives: 29 us -> 0 us
  Pallas kernels: 59.3 us -> 83.1 us
  starting transfers between devices: 10.3 us -> 0.04 us
    pallas_call x3, Pallas kernels: 25.6 us -> 61.7 us  [the longest x1 21.4 us: send_queries(): pl.pallas_call(send_kernel, out_shape=(jax.ShapeDtypeStruct((peers, most,...]
    all_to_all x1 -> x0, blocking collectives: 29 us -> none  [on_device(): lax.all_to_all(payload.reshape(peers, most, -1), 'req', split_axis=0, con...]
    pallas_call x1, Pallas kernels: 33.7 us -> 21.4 us  [prefill_attention(): pl.pallas_call(functools.partial(prefill_kernel, heads), out_shape=jax.Sh...]
    ppermute x7 -> x0, starting transfers between devices: 10.2 us -> none  [on_device(): lax.ppermute(answers[hop], 'req', [(i, (i + hop) % peers) for i in range(...]
  transfers between devices with their start and end apart: 8 -> 1, of which waited for: 1 -> 0; matrix products, arithmetic and copies ran while one was open for 1% -> 1% of each run, Pallas kernels for 48% -> 60%
where the time goes in v3:
time: 103 us; the launch traced here: 102 us
  Pallas kernels  83.1 us (81%)
  between operations  14.1 us (14%)
  local copies, waits for them, and re-layouts  3.99 us (4%)
    pallas_call x1, Pallas kernels, prefill_attention(): pl.pallas_call(functools.partial(prefill_kernel, heads), out_shape=jax.Sh...  21.4 us
    pallas_call x1, Pallas kernels, send_queries(): pl.pallas_call(send_kernel, out_shape=(jax.ShapeDtypeStruct((peers, most,...  21.4 us
    pallas_call x1, Pallas kernels, decode_attention(): pl.pallas_call(functools.partial(decode_kernel, per_step, head_count), ou...  21.2 us
    pallas_call x1, Pallas kernels, return_answers(): pl.pallas_call(collect_kernel, out_shape=jax.ShapeDtypeStruct((back.shape...  19.2 us
  transfers between devices with their start and end apart: 1, of which 0 were waited for; matrix products, arithmetic and copies ran while one was open for 1% of the time, Pallas kernels for 60%

profile of v3, /device:TPU:0, one launch (start us, length us, event | category | flops | bytes accessed | tf_op | source)
XLA Modules:
  0.0 102.1 jit_solution(435036966551407566)
XLA Ops:
  7.2 0.0 all-gather.2.cloned.1.call-start
  7.2 0.7 and_select_fusion.1
  7.9 0.8 copy.15
  8.7 0.1 select_convert_fusion
  8.8 1.9 %concatenate.3 = bf16[128,2176]{1,0:T(8,128)(2,1)} concatenate(bf16[128,1536]{1,0:T(8,128)(2,1)} %param.13, bf16[128,512]{1,0:T(8,128)(2,1)} %param.14, bf16[128,64]{1,0:T(8,128)(2,1)S(1)} %bitcast.3, bf16[128,64]{1,0:T(8,128)(2,1)S(1)} %select_convert_fusion), dimensions={1} | concatenate | bytes 1114112 | tf_op jit(solution)/shard_map/concatenate | solution.py:417
  10.7 0.0 all-gather.2.cloned.1.call-update
  10.7 0.6 broadcast_in_dim_tile.3.frequency_ref
  11.3 21.4 %shard_map.140 = (bf16[8,16,3200]{2,1,0:T(8,128)(2,1)}, s32[1,64]{1,0:T(1,128)}) custom-call(s32[1,64]{1,0:T(1,128)} %bitcast.4, s32[1,64]{1,0:T(1,128)} %bitcast.5, bf16[64,3072]{1,0:T(8,128)(2,1)} %queries_ref.1), custom_call_target="tpu_custom_call" | custom-call | tf_op jit(solution)/shard_map/pallas_call | solution.py:105
  32.7 21.2 %shard_map.141.answers_ref = bf16[8,16,2048]{2,1,0:T(8,128)(2,1)} custom-call(s32[64]{0:T(128)} %lengths_ref.1, bf16[8,16,3200]{2,1,0:T(8,128)(2,1)} %get-tuple-element.5.payload_ref, bf16[512,2048]{1,0:T(8,128)(2,1)} %key_up_ref.3, bf16[512,2048]{1,0:T(8,128)(2,1)} %value_up_ref.3, bf16[64,256,512]{2,1,0:T(8,128)(2,1)} %cache_ref.1, ...), custom_call_target="tpu_custom_call" | custom-call | flops 4831838208 | bytes 17596416 | tf_op jit(solution)/shard_map/pallas_call | solution.py:236
  53.9 19.2 %shard_map.143 = bf16[64,2048]{1,0:T(8,128)(2,1)} custom-call(s32[1,64]{1,0:T(1,128)} %get-tuple-element.7.back_ref, bf16[8,16,2048]{2,1,0:T(8,128)(2,1)} %shard_map.141.answers_ref), custom_call_target="tpu_custom_call" | custom-call | tf_op jit(solution)/shard_map/pallas_call | solution.py:133
  73.1 0.0 copy-start
  73.1 0.0 all-gather.2.cloned.1.call-done.query_latents_ref.latents_ref.extras_ref
  73.1 21.4 %shard_map.142 = bf16[512,2048]{1,0:T(8,128)(2,1)} custom-call(bf16[512,2176]{1,0:T(8,128)(2,1)} %all-gather.2.cloned.1.call-done.query_latents_ref.latents_ref.extras_ref, bf16[512,2176]{1,0:T(8,128)(2,1)} %all-gather.2.cloned.1.call-done.query_latents_ref.latents_ref.extras_ref, ...), custom_call_target="tpu_custom_call" | custom-call | flops 10200547328 | bytes 13631488 | tf_op jit(solution)/shard_map/pallas_call | solution.py:359
  94.5 0.0 copy-done
  94.5 0.7 copy.17
  (3 shorter events, 0.0 us)
Async XLA Ops:
  7.2 66.0 %all-gather.2.cloned.1.call-start = ((), (), s32[]{:S(2)}) async-start(), calls=%async_computation | async-start | bytes 2785280 | tf_op jit(solution)/shard_map/all_gather | solution.py:426
  73.1 21.4 %copy-start = (bf16[64,2048]{1,0:T(8,128)(2,1)S(1)}, bf16[64,2048]{1,0:T(8,128)(2,1)}, u32[]{:S(2)}) copy-start(bf16[64,2048]{1,0:T(8,128)(2,1)} %shard_map.143) | copy-start | bytes 786436
Sparse Core Ops, SparseCore 0:
  10.8 26.0 all-gather.1

commit v4 on v3

--- a/solution.py
+++ b/solution.py
@@ -34,41 +34,49 @@
     return (grown * (1.0 / total)).astype(jnp.bfloat16)
 
 
-def exchange(peers, source_ref, target_ref, local_sem, send_sem, recv_sem):
+def greet(partners):
+    barrier = pltpu.get_barrier_semaphore()
+    for partner in partners:
+        pl.semaphore_signal(
+            barrier, inc=1, device_id=partner, device_id_type=pl.DeviceIdType.MESH
+        )
+    pl.semaphore_wait(barrier, len(partners))
+
+
+def remote(source, target, send_sem, recv_sem, partner):
+    return pltpu.make_async_remote_copy(
+        src_ref=source,
+        dst_ref=target,
+        send_sem=send_sem,
+        recv_sem=recv_sem,
+        device_id=partner,
+        device_id_type=pl.DeviceIdType.MESH,
+    )
+
+
+def peer_at(hop, peers):
+    return lax.rem(lax.axis_index("req") + hop, peers)
+
+
+def exchange_copies(peers, source_ref, target_ref, local_sem, send_sem, recv_sem):
     me = lax.axis_index("req")
-    barrier = pltpu.get_barrier_semaphore()
+    copies = [pltpu.make_async_copy(source_ref.at[me], target_ref.at[me], local_sem)]
     for hop in range(1, peers):
-        pl.semaphore_signal(
-            barrier,
-            inc=1,
-            device_id={"req": lax.rem(me + hop, peers)},
-            device_id_type=pl.DeviceIdType.MESH,
+        target = peer_at(hop, peers)
+        copies.append(
+            remote(
+                source_ref.at[target],
+                target_ref.at[me],
+                send_sem.at[hop],
+                recv_sem.at[hop],
+                {"req": target},
+            )
         )
-    pl.semaphore_wait(barrier, peers - 1)
-    copies = []
-    for hop in range(1, peers):
-        target = lax.rem(me + hop, peers)
-        copy = pltpu.make_async_remote_copy(
-            src_ref=source_ref.at[target],
-            dst_ref=target_ref.at[me],
-            send_sem=send_sem.at[hop],
-            recv_sem=recv_sem.at[hop],
-            device_id={"req": target},
-            device_id_type=pl.DeviceIdType.MESH,
-        )
-        copy.start()
-        copies.append(copy)
-    own = pltpu.make_async_copy(source_ref.at[me], target_ref.at[me], local_sem)
-    own.start()
-    own.wait()
-    for copy in copies:
-        copy.wait()
-
-
-def send_kernel(
-    owner_ref, slot_ref, queries_ref, payload_ref, back_ref, packed_ref, local_sem, send_sem, recv_sem
-):
-    peers, most, _ = payload_ref.shape
+    return copies
+
+
+def pack_queries(owner_ref, slot_ref, queries_ref, back_ref, packed_ref):
+    peers, most, _ = packed_ref.shape
     rows, width = queries_ref.shape
     owner = owner_ref[...].astype(jnp.float32)
     slot = slot_ref[...].astype(jnp.float32)
@@ -88,7 +96,200 @@
     packed_ref[:, :, width:] = (
         jnp.broadcast_to(code, (peers * most, 128)).reshape(peers, most, 128).astype(jnp.bfloat16)
     )
-    exchange(peers, packed_ref, payload_ref, local_sem, send_sem, recv_sem)
+
+
+def pack_extras(rotary_ref, positions_ref, extras_ref):
+    tokens = extras_ref.shape[0]
+    rotary = rotary_ref[...].astype(jnp.float32)
+    place = jnp.broadcast_to(positions_ref[...].astype(jnp.float32), (D_ROPE, tokens))
+    high = jnp.floor(place * (1.0 / DIGIT))
+    row = lax.broadcasted_iota(jnp.int32, (D_ROPE, tokens), 0)
+    digits = jnp.where(row == 0, high, jnp.where(row == 1, place - high * DIGIT, 0.0))
+    extras_ref[...] = jnp.concatenate([rotary, digits], axis=0).T.astype(jnp.bfloat16)
+
+
+def first_kernel(
+    heads,
+    owner_ref,
+    slot_ref,
+    queries_ref,
+    latents_in_ref,
+    query_latents_in_ref,
+    rotary_ref,
+    positions_ref,
+    frequency_ref,
+    query_up_ref,
+    key_up_ref,
+    value_up_ref,
+    payload_ref,
+    back_ref,
+    query_latents_out_ref,
+    latents_out_ref,
+    extras_out_ref,
+    out_ref,
+    packed_ref,
+    extras_in_ref,
+    query_latents_ref,
+    latents_ref,
+    extras_ref,
+    bias_ref,
+    cosine_ref,
+    sine_ref,
+    key_rope_ref,
+    local_sem,
+    send_sem,
+    recv_sem,
+    near_send_sem,
+    near_recv_sem,
+    keep_sem,
+):
+    peers = payload_ref.shape[0]
+    groups = query_latents_ref.shape[0]
+    step = pl.program_id(0)
+    group = lax.axis_index("head")
+    sibling = group + 1 - 2 * lax.rem(group, 2)
+    far = lax.rem(group + groups // 2, groups)
+    gathered = (query_latents_ref, latents_ref, extras_ref)
+    kept = (query_latents_out_ref, latents_out_ref, extras_out_ref)
+
+    def keeping():
+        return [
+            pltpu.make_async_copy(source, target, keep_sem.at[index])
+            for index, (source, target) in enumerate(zip(gathered, kept))
+        ]
+
+    def exchanging():
+        return exchange_copies(peers, packed_ref, payload_ref, local_sem, send_sem, recv_sem)
+
+    @pl.when(step == 0)
+    def _():
+        pack_extras(rotary_ref, positions_ref, extras_in_ref)
+        pack_queries(owner_ref, slot_ref, queries_ref, back_ref, packed_ref)
+        greet(
+            [{"req": peer_at(hop, peers)} for hop in range(1, peers)]
+            + [{"head": sibling}, {"head": far}]
+        )
+        mine = (query_latents_in_ref, latents_in_ref, extras_in_ref)
+        near, across, forward = [], [], []
+        for index, (source, target) in enumerate(zip(mine, gathered)):
+            for kind, (copies, partner) in enumerate(((across, far), (near, sibling))):
+                copies.append(
+                    remote(
+                        source,
+                        target.at[group],
+                        near_send_sem.at[index, kind],
+                        near_recv_sem.at[index, kind],
+                        {"head": partner},
+                    )
+                )
+        for copy in across:
+            copy.start()
+        for copy in near:
+            copy.start()
+        for copy in exchanging():
+            copy.start()
+        for source, target in zip(mine, gathered):
+            target[group] = source[...]
+        for index, (copy, target) in enumerate(zip(across, gathered)):
+            copy.wait_recv()
+            onward = remote(
+                target.at[far],
+                target.at[far],
+                near_send_sem.at[index, 2],
+                near_recv_sem.at[index, 2],
+                {"head": sibling},
+            )
+            onward.start()
+            forward.append(onward)
+        for copy in across:
+            copy.wait_send()
+        for copy in near + forward:
+            copy.wait()
+        for copy in keeping():
+            copy.start()
+        prefill_setup(
+            extras_ref, frequency_ref, bias_ref, cosine_ref, sine_ref, key_rope_ref
+        )
+
+    prefill_heads(
+        heads,
+        query_latents_ref,
+        latents_ref,
+        query_up_ref,
+        key_up_ref,
+        value_up_ref,
+        out_ref,
+        bias_ref,
+        cosine_ref,
+        sine_ref,
+        key_rope_ref,
+    )
+
+    @pl.when(step == pl.num_programs(0) - 1)
+    def _():
+        for copy in keeping() + exchanging():
+            copy.wait()
+
+
+def last_kernel(
+    heads,
+    back_ref,
+    answers_ref,
+    query_latents_ref,
+    latents_ref,
+    extras_ref,
+    frequency_ref,
+    query_up_ref,
+    key_up_ref,
+    value_up_ref,
+    decoded_ref,
+    out_ref,
+    landed_ref,
+    bias_ref,
+    cosine_ref,
+    sine_ref,
+    key_rope_ref,
+    local_sem,
+    send_sem,
+    recv_sem,
+):
+    peers, most, width = landed_ref.shape
+    step = pl.program_id(0)
+
+    def exchanging():
+        return exchange_copies(peers, answers_ref, landed_ref, local_sem, send_sem, recv_sem)
+
+    @pl.when(step == 0)
+    def _():
+        greet([{"req": peer_at(hop, peers)} for hop in range(1, peers)])
+        for copy in exchanging():
+            copy.start()
+        prefill_setup(
+            extras_ref, frequency_ref, bias_ref, cosine_ref, sine_ref, key_rope_ref
+        )
+
+    prefill_heads(
+        heads,
+        query_latents_ref,
+        latents_ref,
+        query_up_ref,
+        key_up_ref,
+        value_up_ref,
+        out_ref,
+        bias_ref,
+        cosine_ref,
+        sine_ref,
+        key_rope_ref,
+    )
+
+    @pl.when(step == pl.num_programs(0) - 1)
+    def _():
+        for copy in exchanging():
+            copy.wait()
+        blocks = landed_ref[...].astype(jnp.float32).reshape(peers * most, width)
+        index = lax.broadcasted_iota(jnp.int32, (peers * most, back_ref.shape[1]), 0)
+        wanted = jnp.where(index == back_ref[...], 1.0, 0.0).astype(jnp.bfloat16)
+        decoded_ref[...] = mm(wanted, blocks.astype(jnp.bfloat16), TN).astype(jnp.bfloat16)
 
 
 def exchange_sems(peers):
@@ -97,49 +298,6 @@
         pltpu.SemaphoreType.DMA((peers,)),
         pltpu.SemaphoreType.DMA((peers,)),
     ]
-
-
-def send_queries(queries, owner, slot, peers, most):
-    rows, width = queries.shape
-    vmem = pl.BlockSpec(memory_space=pltpu.VMEM)
-    return pl.pallas_call(
-        send_kernel,
-        out_shape=(
-            jax.ShapeDtypeStruct((peers, most, width + 128), jnp.bfloat16),
-            jax.ShapeDtypeStruct((1, rows), jnp.int32),
-        ),
-        in_specs=[vmem] * 3,
-        out_specs=(pl.BlockSpec(memory_space=pl.ANY), vmem),
-        scratch_shapes=[pltpu.VMEM((peers, most, width + 128), jnp.bfloat16)]
-        + exchange_sems(peers),
-        compiler_params=pltpu.CompilerParams(
-            vmem_limit_bytes=VMEM_BYTES, collective_id=0, has_side_effects=True
-        ),
-    )(owner[None, :], slot[None, :], queries)
-
-
-def collect_kernel(back_ref, answers_ref, out_ref, landed_ref, local_sem, send_sem, recv_sem):
-    peers, most, width = landed_ref.shape
-    exchange(peers, answers_ref, landed_ref, local_sem, send_sem, recv_sem)
-    blocks = landed_ref[...].astype(jnp.float32).reshape(peers * most, width)
-    index = lax.broadcasted_iota(jnp.int32, (peers * most, back_ref.shape[1]), 0)
-    wanted = jnp.where(index == back_ref[...], 1.0, 0.0).astype(jnp.bfloat16)
-    out_ref[...] = mm(wanted, blocks.astype(jnp.bfloat16), TN).astype(jnp.bfloat16)
-
-
-def return_answers(back, answers):
-    peers = answers.shape[0]
-    vmem = pl.BlockSpec(memory_space=pltpu.VMEM)
-    return pl.pallas_call(
-        collect_kernel,
-        out_shape=jax.ShapeDtypeStruct((back.shape[1], answers.shape[2]), jnp.bfloat16),
-        in_specs=[vmem, pl.BlockSpec(memory_space=pl.ANY)],
-        out_specs=vmem,
-        scratch_shapes=[pltpu.VMEM(answers.shape, jnp.bfloat16)] + exchange_sems(peers),
-        compiler_params=pltpu.CompilerParams(
-            vmem_limit_bytes=VMEM_BYTES, collective_id=1, has_side_effects=True
-        ),
-    )(back, answers)
 
 
 def decode_kernel(
@@ -260,12 +418,42 @@
     )(lengths, payload, key_up, value_up, cache, rope_cache)
 
 
-def prefill_kernel(
+def lane_marks(tokens):
+    lanes = lax.broadcasted_iota(jnp.int32, (tokens, D_NOPE), 1)
+    return lanes < D_ROPE, lanes % D_ROPE < D_ROPE // 2
+
+
+def rotated(values, leading, cosine_ref, sine_ref):
+    swapped = jnp.where(
+        leading,
+        pltpu.roll(values, D_NOPE - D_ROPE // 2, 1),
+        pltpu.roll(values, D_ROPE // 2, 1),
+    )
+    return values * cosine_ref[...] + swapped * sine_ref[...]
+
+
+def prefill_setup(extras_ref, frequency_ref, bias_ref, cosine_ref, sine_ref, key_rope_ref):
+    tokens = bias_ref.shape[0]
+    low, leading = lane_marks(tokens)
+    extras = extras_ref[...].astype(jnp.float32).reshape(tokens, D_NOPE)
+    position = extras[:, D_ROPE : D_ROPE + 1] * DIGIT + extras[:, D_ROPE + 1 : D_ROPE + 2]
+    row = lax.broadcasted_iota(jnp.int32, (tokens, tokens), 0).astype(jnp.float32)
+    column = lax.broadcasted_iota(jnp.int32, (tokens, tokens), 1).astype(jnp.float32)
+    visible = (column <= row) & (column >= row - position)
+    bias_ref[...] = jnp.where(visible, 0.0, MASKED)
+    angles = position * frequency_ref[...]
+    cosine_ref[...] = jnp.cos(angles)
+    sines = jnp.sin(angles)
+    sine_ref[...] = jnp.where(leading, -sines, sines)
+    twice = jnp.where(low, extras, pltpu.roll(extras, D_ROPE, 1))
+    turned = rotated(twice, leading, cosine_ref, sine_ref)
+    key_rope_ref[...] = turned.T[:D_ROPE].astype(jnp.bfloat16)
+
+
+def prefill_heads(
     heads,
     query_latents_ref,
     latents_ref,
-    extras_ref,
-    frequency_ref,
     query_up_ref,
     key_up_ref,
     value_up_ref,
@@ -275,37 +463,13 @@
     sine_ref,
     key_rope_ref,
 ):
-    tokens = query_latents_ref.shape[0]
-    lanes = lax.broadcasted_iota(jnp.int32, (tokens, D_NOPE), 1)
-    low = lanes < D_ROPE
-    leading = lanes % D_ROPE < D_ROPE // 2
-
-    def rotated(values):
-        swapped = jnp.where(
-            leading,
-            pltpu.roll(values, D_NOPE - D_ROPE // 2, 1),
-            pltpu.roll(values, D_ROPE // 2, 1),
-        )
-        return values * cosine_ref[...] + swapped * sine_ref[...]
-
-    @pl.when(pl.program_id(0) == 0)
-    def _():
-        extras = extras_ref[...].astype(jnp.float32)
-        position = extras[:, D_ROPE : D_ROPE + 1] * DIGIT + extras[:, D_ROPE + 1 : D_ROPE + 2]
-        row = lax.broadcasted_iota(jnp.int32, (tokens, tokens), 0).astype(jnp.float32)
-        column = lax.broadcasted_iota(jnp.int32, (tokens, tokens), 1).astype(jnp.float32)
-        visible = (column <= row) & (column >= row - position)
-        bias_ref[...] = jnp.where(visible, 0.0, MASKED)
-        angles = position * frequency_ref[...]
-        cosine_ref[...] = jnp.cos(angles)
-        sines = jnp.sin(angles)
-        sine_ref[...] = jnp.where(leading, -sines, sines)
-        twice = jnp.where(low, extras, pltpu.roll(extras, D_ROPE, 1))
-        key_rope_ref[...] = rotated(twice).T[:D_ROPE].astype(jnp.bfloat16)
-
-    projected = mm(query_latents_ref[...], query_up_ref[...])
-    keys = mm(latents_ref[...], key_up_ref[...]).astype(jnp.bfloat16).T
-    values = mm(latents_ref[...], value_up_ref[...]).astype(jnp.bfloat16)
+    tokens = bias_ref.shape[0]
+    low, leading = lane_marks(tokens)
+    query_latents = query_latents_ref[...].reshape(tokens, query_up_ref.shape[0])
+    latents = latents_ref[...].reshape(tokens, key_up_ref.shape[0])
+    projected = mm(query_latents, query_up_ref[...])
+    keys = mm(latents, key_up_ref[...]).astype(jnp.bfloat16).T
+    values = mm(latents, value_up_ref[...]).astype(jnp.bfloat16)
     key_rope = key_rope_ref[...]
     none = jnp.zeros((D_ROPE, tokens), jnp.bfloat16)
     tile = min(256, tokens)
@@ -314,9 +478,9 @@
         base = pair * 2 * D_Q
         left = projected[:, base : base + D_NOPE].astype(jnp.bfloat16)
         middle = projected[:, base + D_NOPE : base + 2 * D_NOPE]
-        middle = jnp.where(low, rotated(middle), middle).astype(jnp.bfloat16)
+        middle = jnp.where(low, rotated(middle, leading, cosine_ref, sine_ref), middle).astype(jnp.bfloat16)
         right = projected[:, base + 2 * D_NOPE : base + 3 * D_NOPE]
-        right = jnp.where(low, right, rotated(right)).astype(jnp.bfloat16)
+        right = jnp.where(low, right, rotated(right, leading, cosine_ref, sine_ref)).astype(jnp.bfloat16)
         even = keys[2 * pair * D_NOPE : (2 * pair + 1) * D_NOPE]
         odd = keys[(2 * pair + 1) * D_NOPE : (2 * pair + 2) * D_NOPE]
         both = (
@@ -345,50 +509,110 @@
         scores = following
 
 
-def prefill_attention(gathered, query_up, key_up, value_up):
-    tokens = gathered.shape[0]
-    latent_width = query_up.shape[0]
-    head_count = key_up.shape[1] // D_NOPE
-    extra_block = (latent_width + D_C) // D_NOPE
-    heads = 4
-    half_width = D_ROPE // 2
-    frequency = ROPE_BASE ** (-jnp.arange(half_width, dtype=jnp.float32) / half_width)
-    whole = lambda step: (0, 0)
-    across = lambda step: (0, step)
-    flops = 2 * tokens * head_count * (latent_width * D_Q + 2 * D_C * D_NOPE + tokens * 384)
+def prefill_scratch(tokens):
+    return [
+        pltpu.VMEM((tokens, tokens), jnp.float32),
+        pltpu.VMEM((tokens, D_NOPE), jnp.float32),
+        pltpu.VMEM((tokens, D_NOPE), jnp.float32),
+        pltpu.VMEM((D_ROPE, tokens), jnp.bfloat16),
+    ]
+
+
+def weight_specs(heads, start, query_latent_width):
+    across = lambda step: (0, step + start)
+    return [
+        pl.BlockSpec((query_latent_width, heads * D_Q), across),
+        pl.BlockSpec((D_C, heads * D_NOPE), across),
+        pl.BlockSpec((D_C, heads * D_V), across),
+    ]
+
+
+def first_call(
+    owner, slot, queries, latents, query_latents, rotary, positions, frequency, weights, split, most
+):
+    peers, groups = lax.axis_size("req"), lax.axis_size("head")
+    heads, steps, _ = split
+    rows, width = queries.shape
+    part, query_latent_width = query_latents.shape
+    tokens = part * groups
+    vmem = pl.BlockSpec(memory_space=pltpu.VMEM)
+    remote_space = pl.BlockSpec(memory_space=pl.ANY)
+    packed = (peers, most, width + 128)
+    gathered = [
+        (groups, part, query_latent_width),
+        (groups, part, D_C),
+        (groups, part, D_NOPE),
+    ]
     return pl.pallas_call(
-        functools.partial(prefill_kernel, heads),
-        out_shape=jax.ShapeDtypeStruct((tokens, head_count * D_V), jnp.bfloat16),
-        grid=(head_count // heads,),
-        in_specs=[
-            pl.BlockSpec((tokens, latent_width), whole),
-            pl.BlockSpec((tokens, D_C), lambda step: (0, latent_width // D_C)),
-            pl.BlockSpec((tokens, D_NOPE), lambda step: (0, extra_block)),
-            pl.BlockSpec((1, D_NOPE), whole),
-            pl.BlockSpec((latent_width, heads * D_Q), across),
-            pl.BlockSpec((D_C, heads * D_NOPE), across),
-            pl.BlockSpec((D_C, heads * D_V), across),
+        functools.partial(first_kernel, heads),
+        out_shape=(
+            jax.ShapeDtypeStruct(packed, jnp.bfloat16),
+            jax.ShapeDtypeStruct((1, rows), jnp.int32),
+            *(jax.ShapeDtypeStruct(shape, jnp.bfloat16) for shape in gathered),
+            jax.ShapeDtypeStruct((tokens, steps * heads * D_V), jnp.bfloat16),
+        ),
+        grid=(steps,),
+        in_specs=[vmem] * 8 + weight_specs(heads, 0, query_latent_width),
+        out_specs=(
+            remote_space,
+            vmem,
+            remote_space,
+            remote_space,
+            remote_space,
+            pl.BlockSpec((tokens, heads * D_V), lambda step: (0, step)),
+        ),
+        scratch_shapes=[
+            pltpu.VMEM(packed, jnp.bfloat16),
+            pltpu.VMEM((part, D_NOPE), jnp.bfloat16),
+            *(pltpu.VMEM(shape, jnp.bfloat16) for shape in gathered),
+            *prefill_scratch(tokens),
+            *exchange_sems(peers),
+            pltpu.SemaphoreType.DMA((3, 3)),
+            pltpu.SemaphoreType.DMA((3, 3)),
+            pltpu.SemaphoreType.DMA((3,)),
         ],
-        out_specs=pl.BlockSpec((tokens, heads * D_V), across),
-        scratch_shapes=[
-            pltpu.VMEM((tokens, tokens), jnp.float32),
-            pltpu.VMEM((tokens, D_NOPE), jnp.float32),
-            pltpu.VMEM((tokens, D_NOPE), jnp.float32),
-            pltpu.VMEM((D_ROPE, tokens), jnp.bfloat16),
-        ],
-        compiler_params=pltpu.CompilerParams(vmem_limit_bytes=VMEM_BYTES),
-        cost_estimate=pl.CostEstimate(
-            flops=flops, bytes_accessed=query_up.size * 2 + key_up.size * 4, transcendentals=0
+        compiler_params=pltpu.CompilerParams(
+            vmem_limit_bytes=VMEM_BYTES, collective_id=0, has_side_effects=True
         ),
     )(
-        gathered,
-        gathered,
-        gathered,
-        jnp.tile(frequency, 4)[None, :],
-        query_up,
-        key_up,
-        value_up,
-    )
+        owner[None, :],
+        slot[None, :],
+        queries,
+        latents,
+        query_latents,
+        rotary,
+        positions[None, :],
+        frequency,
+        *weights,
+    )
+
+
+def last_call(back, answers, gathered, frequency, weights, split):
+    peers = answers.shape[0]
+    heads, steps, start = split
+    groups, part, query_latent_width = gathered[0].shape
+    tokens = groups * part
+    vmem = pl.BlockSpec(memory_space=pltpu.VMEM)
+    return pl.pallas_call(
+        functools.partial(last_kernel, heads),
+        out_shape=(
+            jax.ShapeDtypeStruct((back.shape[1], answers.shape[2]), jnp.bfloat16),
+            jax.ShapeDtypeStruct((tokens, steps * heads * D_V), jnp.bfloat16),
+        ),
+        grid=(steps,),
+        in_specs=[vmem, pl.BlockSpec(memory_space=pl.ANY)]
+        + [vmem] * 4
+        + weight_specs(heads, start, query_latent_width),
+        out_specs=(vmem, pl.BlockSpec((tokens, heads * D_V), lambda step: (0, step))),
+        scratch_shapes=[
+            pltpu.VMEM(answers.shape, jnp.bfloat16),
+            *prefill_scratch(tokens),
+            *exchange_sems(peers),
+        ],
+        compiler_params=pltpu.CompilerParams(
+            vmem_limit_bytes=VMEM_BYTES, collective_id=1, has_side_effects=True
+        ),
+    )(back, answers, *gathered, frequency, *weights)
 
 
 def on_device(
@@ -407,26 +631,29 @@
     cache_live_lengths,
 ):
     row_count = decode_queries.shape[0]
-    token_count = prompt_latents.shape[0]
     peers = lax.axis_size("req")
     most = max(2, row_count * 2 // peers)
-
-    lane = lax.broadcasted_iota(jnp.int32, (token_count, D_ROPE), 1)
-    place = positions[:, None]
-    digits = jnp.where(lane == 0, place // DIGIT, jnp.where(lane == 1, place % DIGIT, 0))
-    prompt = jnp.concatenate(
-        [
-            prompt_query_latents,
-            prompt_latents,
-            prompt_rotary_keys.T,
-            digits.astype(jnp.bfloat16),
-        ],
-        axis=1,
-    )
-    prompt = lax.all_gather(prompt, "head", axis=0, tiled=True)
-
-    payload, back = send_queries(
-        decode_queries, decode_owner_index, decode_cache_slot, peers, most
+    half_width = D_ROPE // 2
+    frequency = ROPE_BASE ** (-jnp.arange(half_width, dtype=jnp.float32) / half_width)
+    frequency = jnp.tile(frequency, 4)[None, :]
+    weights = (query_up_weight, key_up_weight, value_up_weight)
+    head_count = key_up_weight.shape[1] // D_NOPE
+    heads = 4
+    steps = head_count // heads
+    early = steps // 2
+
+    payload, back, *gathered, first_half = first_call(
+        decode_owner_index,
+        decode_cache_slot,
+        decode_queries,
+        prompt_latents,
+        prompt_query_latents,
+        prompt_rotary_keys,
+        positions,
+        frequency,
+        weights,
+        (heads, early, 0),
+        most,
     )
     answers = decode_attention(
         payload,
@@ -436,12 +663,10 @@
         rotated_cache_keys,
         cache_live_lengths,
     )
-    decode_out = return_answers(back, answers)
-    prompt, _ = lax.optimization_barrier((prompt, answers))
-    prompt_attention_output = prefill_attention(
-        prompt, query_up_weight, key_up_weight, value_up_weight
-    )
-    return (prompt_attention_output, decode_out)
+    decode_out, second_half = last_call(
+        back, answers, gathered, frequency, weights, (heads, steps - early, early)
+    )
+    return (jnp.concatenate([first_half, second_half], axis=1), decode_out)
 
 
 def solution(mesh):

time: 103 us -> 78 us (0.76)
  between operations: 14.1 us -> 0.68 us
  Pallas kernels: 83.1 us -> 72.5 us
  local copies, waits for them, and re-layouts: 3.99 us -> 1.31 us
  other arithmetic: 0.79 us -> 2.82 us
    pallas_call x3 -> x2, Pallas kernels: 61.9 us -> 51.3 us  [the longest x1 34.3 us: first_call(): pl.pallas_call(functools.partial(first_kernel, heads), out_shape=(jax.Sha...]
    concatenate x0 -> x1, other arithmetic: none -> 2.81 us  [on_device(): return (jnp.concatenate([first_half, second_half], axis=1), decode_out)]
    concatenate x1 -> x0, local copies, waits for them, and re-layouts: 1.86 us -> none  [on_device(): jnp.concatenate([prompt_query_latents, prompt_latents, prompt_rotary_keys...]
  transfers between devices with their start and end apart: 1 -> 0, of which waited for: 0 -> 0; matrix products, arithmetic and copies ran while one was open for 1% -> 0% of each run, Pallas kernels for 60% -> 0%
where the time goes in v4:
time: 78 us; the launch traced here: 77.3 us
  Pallas kernels  72.5 us (93%)
  other arithmetic  2.82 us (4%)
  local copies, waits for them, and re-layouts  1.31 us (2%)
    pallas_call x1, Pallas kernels, first_call(): pl.pallas_call(functools.partial(first_kernel, heads), out_shape=(jax.Sha...  34.3 us
    pallas_call x1, Pallas kernels, decode_attention(): pl.pallas_call(functools.partial(decode_kernel, per_step, head_count), ou...  21.2 us
    pallas_call x1, Pallas kernels, last_call(): pl.pallas_call(functools.partial(last_kernel, heads), out_shape=(jax.Shap...  17 us
    concatenate x1, other arithmetic, on_device(): return (jnp.concatenate([first_half, second_half], axis=1), decode_out)  2.81 us

profile of v4, /device:TPU:0, one launch (start us, length us, event | category | flops | bytes accessed | tf_op | source)
XLA Modules:
  0.0 77.3 jit_solution(8035237787107554263)
XLA Ops:
  0.7 0.6 broadcast_in_dim_tile.5.frequency_ref
  1.2 34.3 %shard_map.140 = (bf16[8,16,3200]{2,1,0:T(8,128)(2,1)}, s32[1,64]{1,0:T(1,128)}, bf16[4,128,1536]{2,1,0:T(8,128)(2,1)}, bf16[4,128,512]{2,1,0:T(8,128)(2,1)}, bf...) custom-call(s32[1,64]{1,0:T(1,128)} %bitcast.3, s32[1,64]{1,0:T(1,128)} %bitcast.4, bf16[64,3072]{1,0:T(8,128)(2,1)} %queries_ref.1, ...), custom_call_target="tpu_custom_call" | custom-call | tf_op jit(solution)/shard_map/pallas_call | solution.py:546
  35.6 21.2 %shard_map.141.answers_ref = bf16[8,16,2048]{2,1,0:T(8,128)(2,1)} custom-call(s32[64]{0:T(128)} %lengths_ref.1, bf16[8,16,3200]{2,1,0:T(8,128)(2,1)} %get-tuple-element.12.payload_ref, bf16[512,2048]{1,0:T(8,128)(2,1)} %key_up_ref.5, bf16[512,2048]{1,0:T(8,128)(2,1)} %value_up_ref.5, bf16[64,256,512]{2,1,0:T(8,128)(2,1)} %cache_ref.1, ...), custom_call_target="tpu_custom_call" | custom-call | flops 4831838208 | bytes 17596416 | tf_op jit(solution)/shard_map/pallas_call | solution.py:394
  56.8 0.0 copy-start
  56.8 17.0 %shard_map.142 = (bf16[64,2048]{1,0:T(8,128)(2,1)}, bf16[512,1024]{1,0:T(8,128)(2,1)}) custom-call(s32[1,64]{1,0:T(1,128)} %get-tuple-element.11.back_ref, bf16[8,16,2048]{2,1,0:T(8,128)(2,1)} %shard_map.141.answers_ref, bf16[4,128,1536]{2,1,0:T(8,128)(2,1)} %get-tuple-element.13.query_latents_ref, bf16[4,128,512]{2,1,0:T(8,128)(2,1)} %get-tuple-element.14.latents_ref, ...), custom_call_target="tpu_custom_call" | custom-call | tf_op jit(solution)/shard_map/pallas_call | solution.py:596
  73.8 0.0 copy-done
  73.8 0.0 copy-start.1
  73.8 2.8 %pad_maximum_fusion = bf16[512,2048]{1,0:T(8,128)(2,1)} fusion(bf16[512,1024]{1,0:T(8,128)(2,1)} %get-tuple-element.16, bf16[512,1024]{1,0:T(8,128)(2,1)S(1)} %copy-done), kind=kLoop, calls=%fused_computation | loop fusion | flops 4194304 | bytes 4194304 | tf_op jit(solution)/shard_map/concatenate | solution.py:669
  76.6 0.0 copy-done.1
  76.6 0.7 copy.16
  (2 shorter events, 0.0 us)
Async XLA Ops:
  56.8 17.0 %copy-start = (bf16[512,1024]{1,0:T(8,128)(2,1)S(1)}, bf16[512,1024]{1,0:T(8,128)(2,1)}, u32[]{:S(2)}) copy-start(bf16[512,1024]{1,0:T(8,128)(2,1)} %get-tuple-element.10) | copy-start | bytes 3145732
  73.8 2.8 %copy-start.1 = (bf16[64,2048]{1,0:T(8,128)(2,1)S(1)}, bf16[64,2048]{1,0:T(8,128)(2,1)}, u32[]{:S(2)}) copy-start(bf16[64,2048]{1,0:T(8,128)(2,1)} %get-tuple-element.21) | copy-start | bytes 786436

commit v5 on v4

--- a/solution.py
+++ b/solution.py
@@ -20,7 +20,7 @@
 DIGIT = 256
 NT = (((1,), (1,)), ((), ()))
 TN = (((0,), (0,)), ((), ()))
-VMEM_BYTES = 56 * 1024 * 1024
+VMEM_BYTES = 40 * 1024 * 1024
 
 
 def mm(a, b, dims=(((1,), (0,)), ((), ()))):
@@ -170,7 +170,7 @@
             + [{"head": sibling}, {"head": far}]
         )
         mine = (query_latents_in_ref, latents_in_ref, extras_in_ref)
-        near, across, forward = [], [], []
+        near, across = [], []
         for index, (source, target) in enumerate(zip(mine, gathered)):
             for kind, (copies, partner) in enumerate(((across, far), (near, sibling))):
                 copies.append(
@@ -182,16 +182,18 @@
                         {"head": partner},
                     )
                 )
-        for copy in across:
+        for copy in across[::-1]:
             copy.start()
-        for copy in near:
+        for copy in near[::-1]:
             copy.start()
         for copy in exchanging():
             copy.start()
         for source, target in zip(mine, gathered):
             target[group] = source[...]
-        for index, (copy, target) in enumerate(zip(across, gathered)):
-            copy.wait_recv()
+
+        def pass_on(index):
+            target = gathered[index]
+            across[index].wait_recv()
             onward = remote(
                 target.at[far],
                 target.at[far],
@@ -200,16 +202,21 @@
                 {"head": sibling},
             )
             onward.start()
-            forward.append(onward)
+            return onward
+
+        forward = pass_on(2)
+        near[2].wait()
+        forward.wait()
+        prefill_setup(
+            extras_ref, frequency_ref, bias_ref, cosine_ref, sine_ref, key_rope_ref
+        )
+        forward = [pass_on(1), pass_on(0)]
         for copy in across:
             copy.wait_send()
-        for copy in near + forward:
+        for copy in near[:2] + forward:
             copy.wait()
         for copy in keeping():
             copy.start()
-        prefill_setup(
-            extras_ref, frequency_ref, bias_ref, cosine_ref, sine_ref, key_rope_ref
-        )
 
     prefill_heads(
         heads,
@@ -313,8 +320,13 @@
     query_ref,
     rope_query_ref,
     latent_out_ref,
+    value_ref,
 ):
     step = pl.program_id(0)
+    value_width = value_up_ref.shape[1]
+    value_ref[:, pl.ds(pl.multiple_of(step * value_width, value_width), value_width)] = (
+        value_up_ref[...]
+    )
     width = head_count * D_Q
     slot_count = query_ref.shape[1] // head_count
     chunks = query_ref.shape[0]
@@ -341,32 +353,44 @@
             rope = queries[:, head * D_Q + D_NOPE : (head + 1) * D_Q]
             rope_query_ref[place, :] = jnp.concatenate([rope, rope], axis=1)
 
-    first = pl.multiple_of(step * slots_per_step, slots_per_step)
-    here = pl.ds(pl.multiple_of(step * rows, rows), rows)
-    columns = jnp.concatenate(
-        [query_ref[chunk, here, :].T for chunk in range(chunks)], axis=0
-    ).astype(jnp.bfloat16)
-    rope_query = rope_query_ref[here, :D_ROPE].astype(jnp.bfloat16)
-    owner = lax.broadcasted_iota(jnp.int32, columns.shape, 1) // head_count
-    none = jnp.zeros_like(columns)
-    turned = None
-    for item in range(slots_per_step):
-        part = mm(cache_ref[item], jnp.where(owner == item, columns, none))
-        turned = part if turned is None else turned + part
-    scores = turned.T
-    lanes = lax.broadcasted_iota(jnp.int32, (head_count, cache_ref.shape[1]), 1)
-    parts = []
-    for item in range(slots_per_step):
-        place = slice(item * head_count, (item + 1) * head_count)
-        part = scores[place] + mm(rope_query[place], rope_ref[item])
-        parts.append(jnp.where(lanes < lengths_ref[first + item], part, MASKED))
-    weights = softmax_weights(jnp.concatenate(parts, axis=0))
-    for item in range(slots_per_step):
-        place = slice(item * head_count, (item + 1) * head_count)
-        latent = mm(weights[place], cache_ref[item]).astype(jnp.bfloat16).astype(jnp.float32)
-        below = pl.ds(pl.multiple_of(step * rows, rows) + item * head_count, head_count)
+    first = step * slots_per_step
+    unit = 128 // head_count
+    cache_rows = cache_ref.shape[1]
+    lanes = lax.broadcasted_iota(jnp.int32, (head_count, cache_rows), 1)
+    owner = lax.broadcasted_iota(jnp.int32, (cache_rows, 128), 1) // head_count
+    batches = range(0, slots_per_step, unit)
+    products = []
+    for batch in batches:
+        here = pl.ds(pl.multiple_of(step * rows, 128) + batch * head_count, 128)
+        columns = jnp.concatenate(
+            [query_ref[chunk, here, :].T for chunk in range(chunks)], axis=0
+        ).astype(jnp.bfloat16)
+        latents = cache_ref[batch : batch + unit].reshape(unit * cache_rows, D_C)
+        products.append(mm(latents, columns))
+    for batch, product in zip(batches, products):
+        here = pl.ds(pl.multiple_of(step * rows, 128) + batch * head_count, 128)
+        turned = product[:cache_rows]
+        for item in range(1, unit):
+            place = slice(item * cache_rows, (item + 1) * cache_rows)
+            turned = jnp.where(owner == item, product[place], turned)
+        scores = turned.T
+        rope_query = rope_query_ref[here, :D_ROPE].astype(jnp.bfloat16)
+        parts = []
+        for item in range(unit):
+            place = slice(item * head_count, (item + 1) * head_count)
+            part = scores[place] + mm(rope_query[place], rope_ref[batch + item])
+            parts.append(jnp.where(lanes < lengths_ref[first + batch + item], part, MASKED))
+        weights = softmax_weights(jnp.concatenate(parts, axis=0))
+        latent = jnp.concatenate(
+            [
+                mm(weights[item * head_count : (item + 1) * head_count], cache_ref[batch + item])
+                for item in range(unit)
+            ],
+            axis=0,
+        )
+        latent = latent.astype(jnp.bfloat16).astype(jnp.float32)
         for chunk in range(chunks):
-            latent_out_ref[chunk, below, :] = latent[:, chunk * 128 : (chunk + 1) * 128]
+            latent_out_ref[chunk, here, :] = latent[:, chunk * 128 : (chunk + 1) * 128]
 
     @pl.when(step == pl.num_programs(0) - 1)
     def _():
@@ -377,7 +401,7 @@
                 [latent_out_ref[chunk, strided, :] for chunk in range(chunks)], axis=1
             )
             place = slice(head * D_V, (head + 1) * D_V)
-            answer = mm(latent.astype(jnp.bfloat16), value_up_ref[:, place])
+            answer = mm(latent.astype(jnp.bfloat16), value_ref[:, place])
             answer = mm(sending, answer.astype(jnp.bfloat16)).astype(jnp.bfloat16)
             out_ref[:, :, place] = answer.reshape(peers, most, D_V)
 
@@ -385,7 +409,8 @@
 def decode_attention(payload, key_up, value_up, cache, rope_cache, lengths):
     slot_count, cache_rows, _ = cache.shape
     head_count = key_up.shape[1] // D_NOPE
-    per_step = 8
+    per_step = 16
+    steps = slot_count // per_step
     peers, most, _ = payload.shape
     whole = lambda step, *_: (0, 0)
     single = lambda step, *_: (0, 0, 0)
@@ -396,11 +421,11 @@
         out_shape=block,
         grid_spec=pltpu.PrefetchScalarGridSpec(
             num_scalar_prefetch=1,
-            grid=(slot_count // per_step,),
+            grid=(steps,),
             in_specs=[
                 pl.BlockSpec(payload.shape, single),
                 pl.BlockSpec(key_up.shape, whole),
-                pl.BlockSpec(value_up.shape, whole),
+                pl.BlockSpec((D_C, value_up.shape[1] // steps), lambda step, *_: (0, step)),
                 pl.BlockSpec((per_step, cache_rows, D_C), lambda step, *_: (step, 0, 0)),
                 pl.BlockSpec((per_step, D_ROPE, cache_rows), lambda step, *_: (step, 0, 0)),
             ],
@@ -409,6 +434,7 @@
                 pltpu.VMEM((D_C // 128, slot_count * head_count, 128), jnp.float32),
                 pltpu.VMEM((slot_count * head_count, 2 * D_ROPE), jnp.float32),
                 pltpu.VMEM((D_C // 128, slot_count * head_count, 128), jnp.float32),
+                pltpu.VMEM(value_up.shape, jnp.bfloat16),
             ],
         ),
         compiler_params=pltpu.CompilerParams(vmem_limit_bytes=VMEM_BYTES),
@@ -615,6 +641,41 @@
     )(back, answers, *gathered, frequency, *weights)
 
 
+def join_kernel(first_ref, second_ref, decoded_ref, out_ref, decoded_out_ref):
+    @pl.when(pl.program_id(0) == 0)
+    def _():
+        out_ref[...] = first_ref[...]
+        decoded_out_ref[...] = decoded_ref[...]
+
+    @pl.when(pl.program_id(0) > 0)
+    def _():
+        out_ref[...] = second_ref[...]
+
+
+def join(first, second, decoded):
+    tokens, width = first.shape
+    total = width + second.shape[1]
+    whole = lambda step: (0, 0)
+    return pl.pallas_call(
+        join_kernel,
+        out_shape=(
+            jax.ShapeDtypeStruct((tokens, total), jnp.bfloat16),
+            jax.ShapeDtypeStruct(decoded.shape, jnp.bfloat16),
+        ),
+        grid=(total // width,),
+        in_specs=[
+            pl.BlockSpec((tokens, width), whole),
+            pl.BlockSpec((tokens, width), lambda step: (0, jnp.maximum(step - 1, 0))),
+            pl.BlockSpec(decoded.shape, whole),
+        ],
+        out_specs=(
+            pl.BlockSpec((tokens, width), lambda step: (0, step)),
+            pl.BlockSpec(decoded.shape, whole),
+        ),
+        compiler_params=pltpu.CompilerParams(vmem_limit_bytes=VMEM_BYTES),
+    )(first, second, decoded)
+
+
 def on_device(
     prompt_query_latents,
     prompt_latents,
@@ -640,7 +701,7 @@
     head_count = key_up_weight.shape[1] // D_NOPE
     heads = 4
     steps = head_count // heads
-    early = steps // 2
+    early = max(1, steps // 4)
 
     payload, back, *gathered, first_half = first_call(
         decode_owner_index,
@@ -666,7 +727,7 @@
     decode_out, second_half = last_call(
         back, answers, gathered, frequency, weights, (heads, steps - early, early)
     )
-    return (jnp.concatenate([first_half, second_half], axis=1), decode_out)
+    return join(first_half, second_half, decode_out)
 
 
 def solution(mesh):

time: 78 us -> 76.5 us (0.981)
  local copies, waits for them, and re-layouts: 1.31 us -> 8.86 us
  Pallas kernels: 72.5 us -> 66.5 us
  other arithmetic: 2.82 us -> 0.01 us
    unnamed x5 -> x26, local copies, waits for them, and re-layouts: 0.71 us -> 8.77 us
    pallas_call x1, Pallas kernels: 34.3 us -> 28.2 us  [first_call(): pl.pallas_call(functools.partial(first_kernel, heads), out_shape=(jax.Sha...]
    pallas_call x1, Pallas kernels: 21.2 us -> 17.8 us  [decode_attention(): pl.pallas_call(functools.partial(decode_kernel, per_step, head_count), ou...]
    concatenate x1 -> x0, other arithmetic: 2.81 us -> none  [on_device(): return (jnp.concatenate([first_half, second_half], axis=1), decode_out)]
    pallas_call x0 -> x1, Pallas kernels: none -> 2.06 us  [join(): pl.pallas_call(join_kernel, out_shape=(jax.ShapeDtypeStruct((tokens, tota...]
    pallas_call x1, Pallas kernels: 17 us -> 18.4 us  [last_call(): pl.pallas_call(functools.partial(last_kernel, heads), out_shape=(jax.Shap...]
where the time goes in v5:
time: 76.5 us; the launch traced here: 76.1 us
  Pallas kernels  66.5 us (87%)
  local copies, waits for them, and re-layouts  8.86 us (12%)
    pallas_call x1, Pallas kernels, first_call(): pl.pallas_call(functools.partial(first_kernel, heads), out_shape=(jax.Sha...  28.2 us
    pallas_call x1, Pallas kernels, last_call(): pl.pallas_call(functools.partial(last_kernel, heads), out_shape=(jax.Shap...  18.4 us
    pallas_call x1, Pallas kernels, decode_attention(): pl.pallas_call(functools.partial(decode_kernel, per_step, head_count), ou...  17.8 us
    unnamed x26, local copies, waits for them, and re-layouts  8.77 us
    pallas_call x1, Pallas kernels, join(): pl.pallas_call(join_kernel, out_shape=(jax.ShapeDtypeStruct((tokens, tota...  2.06 us

profile of v5, /device:TPU:0, one launch (start us, length us, event | category | flops | bytes accessed | tf_op | source)
XLA Modules:
  0.0 76.1 jit_solution(7362231839580736081)
XLA Ops:
  0.7 0.1 broadcast_in_dim_tile.5.frequency_ref
  0.7 0.0 copy-start
  0.7 1.6 %copy-done = bf16[512,2048]{1,0:T(8,128)(2,1)S(1)} copy-done((bf16[512,2048]{1,0:T(8,128)(2,1)S(1)}, bf16[512,2048]{1,0:T(8,128)(2,1)}, u32[]{:S(2)}) %copy-start) | copy-done | bytes 2097176
  2.3 0.0 copy-start.2
  2.3 1.6 %copy-done.2 = bf16[512,2048]{1,0:T(8,128)(2,1)S(1)} copy-done((bf16[512,2048]{1,0:T(8,128)(2,1)S(1)}, bf16[512,2048]{1,0:T(8,128)(2,1)}, u32[]{:S(2)}) %copy-start.2) | copy-done | bytes 2097176
  3.9 0.0 copy-start.5
  3.9 1.0 %copy-done.5 = bf16[64,3072]{1,0:T(8,128)(2,1)S(1)} copy-done((bf16[64,3072]{1,0:T(8,128)(2,1)S(1)}, bf16[64,3072]{1,0:T(8,128)(2,1)}, u32[]{:S(2)}) %copy-start.5) | copy-done | bytes 393240
  4.9 0.0 copy-start.6
  4.9 1.0 %copy-done.6 = bf16[128,1536]{1,0:T(8,128)(2,1)S(1)} copy-done((bf16[128,1536]{1,0:T(8,128)(2,1)S(1)}, bf16[128,1536]{1,0:T(8,128)(2,1)}, u32[]{:S(2)}) %copy-start.6) | copy-done | bytes 393240
  5.9 0.0 copy-start.7
  5.9 0.9 %copy-done.7 = bf16[128,512]{1,0:T(8,128)(2,1)S(1)} copy-done((bf16[128,512]{1,0:T(8,128)(2,1)S(1)}, bf16[128,512]{1,0:T(8,128)(2,1)}, u32[]{:S(2)}) %copy-start.7) | copy-done | bytes 131096
  6.8 0.0 copy-start.8
  6.8 0.7 copy-done.8
  7.5 0.7 copy-done.9
  8.2 0.7 copy-done.10
  8.9 0.7 copy-done.11
  9.5 28.2 %shard_map.140 = (bf16[8,16,3200]{2,1,0:T(8,128)(2,1)S(1)}, s32[1,64]{1,0:T(1,128)S(1)}, bf16[4,128,1536]{2,1,0:T(8,128)(2,1)S(1)}, bf16[4,128,512]{2,1,0:T(8,12...) custom-call(s32[1,64]{1,0:T(1,128)S(1)} %bitcast.3, s32[1,64]{1,0:T(1,128)S(1)} %bitcast.4, ...), custom_call_target="tpu_custom_call" | custom-call | tf_op jit(solution)/shard_map/pallas_call | solution.py:572
  37.7 0.0 copy-done.1
  37.7 0.0 copy-done.3
  37.7 0.0 copy-done.4
  37.7 0.0 copy-done.12
  37.7 17.8 %shard_map.141.answers_ref = bf16[8,16,2048]{2,1,0:T(8,128)(2,1)S(1)} custom-call(s32[64]{0:T(128)S(1)} %copy-done.12, bf16[8,16,3200]{2,1,0:T(8,128)(2,1)S(1)} %get-tuple-element.12.payload_ref, bf16[512,2048]{1,0:T(8,128)(2,1)S(1)} %copy-done.1, bf16[512,2048]{1,0:T(8,128)(2,1)S(1)} %copy-done.3, bf16[64,256,512]{2,1,0:T(8,128)(2,1)} %cache_ref.1, ...), custom_call_target="tpu_custom_call" | custom-call | flops 4831838208 | bytes 17596416 | tf_op jit(solution)/shard_map/pallas_call | solution.py:419
  55.6 18.4 %shard_map.142 = (bf16[64,2048]{1,0:T(8,128)(2,1)S(1)}, bf16[512,1536]{1,0:T(8,128)(2,1)S(1)}) custom-call(s32[1,64]{1,0:T(1,128)S(1)} %get-tuple-element.11.back_ref, bf16[8,16,2048]{2,1,0:T(8,128)(2,1)S(1)} %shard_map.141.answers_ref, bf16[4,128,1536]{2,1,0:T(8,128)(2,1)S(1)} %get-tuple-element.13.query_latents_ref, ...), custom_call_target="tpu_custom_call" | custom-call | tf_op jit(solution)/shard_map/pallas_call | solution.py:622
  74.0 2.1 %shard_map.143 = (bf16[512,2048]{1,0:T(8,128)(2,1)}, bf16[64,2048]{1,0:T(8,128)(2,1)}) custom-call(bf16[512,512]{1,0:T(8,128)(2,1)S(1)} %get-tuple-element.10.first_ref, bf16[512,1536]{1,0:T(8,128)(2,1)S(1)} %get-tuple-element.16.second_ref, bf16[64,2048]{1,0:T(8,128)(2,1)S(1)} %get-tuple-element.17.decoded_ref), custom_call_target="tpu_custom_call" | custom-call | tf_op jit(solution)/shard_map/pallas_call | solution.py:659
  (9 shorter events, 0.0 us)
Async XLA Ops:
  0.7 1.6 %copy-start = (bf16[512,2048]{1,0:T(8,128)(2,1)S(1)}, bf16[512,2048]{1,0:T(8,128)(2,1)}, u32[]{:S(2)}) copy-start(bf16[512,2048]{1,0:T(8,128)(2,1)} %key_up_ref.5) | copy-start | bytes 6291460
  2.3 1.6 %copy-start.2 = (bf16[512,2048]{1,0:T(8,128)(2,1)S(1)}, bf16[512,2048]{1,0:T(8,128)(2,1)}, u32[]{:S(2)}) copy-start(bf16[512,2048]{1,0:T(8,128)(2,1)} %value_up_ref.5) | copy-start | bytes 6291460
  3.9 1.0 %copy-start.5 = (bf16[64,3072]{1,0:T(8,128)(2,1)S(1)}, bf16[64,3072]{1,0:T(8,128)(2,1)}, u32[]{:S(2)}) copy-start(bf16[64,3072]{1,0:T(8,128)(2,1)} %queries_ref.1) | copy-start | bytes 1179652
  4.9 1.0 %copy-start.6 = (bf16[128,1536]{1,0:T(8,128)(2,1)S(1)}, bf16[128,1536]{1,0:T(8,128)(2,1)}, u32[]{:S(2)}) copy-start(bf16[128,1536]{1,0:T(8,128)(2,1)} %query_latents_in_ref.1) | copy-start | bytes 1179652
  5.9 0.9 %copy-start.7 = (bf16[128,512]{1,0:T(8,128)(2,1)S(1)}, bf16[128,512]{1,0:T(8,128)(2,1)}, u32[]{:S(2)}) copy-start(bf16[128,512]{1,0:T(8,128)(2,1)} %latents_in_ref.1) | copy-start | bytes 393220
  6.8 0.7 copy-start.8
  7.5 0.7 copy-start.9
  8.2 0.7 copy-start.10
  8.8 0.7 copy-start.11
  9.5 28.2 %copy-start.1 = (bf16[512,2048]{1,0:T(8,128)(2,1)S(1)}, bf16[512,2048]{1,0:T(8,128)(2,1)}, u32[]{:S(2)}) copy-start(bf16[512,2048]{1,0:T(8,128)(2,1)} %key_up_ref.5) | copy-start | bytes 6291460
  9.5 28.2 %copy-start.3 = (bf16[512,2048]{1,0:T(8,128)(2,1)S(1)}, bf16[512,2048]{1,0:T(8,128)(2,1)}, u32[]{:S(2)}) copy-start(bf16[512,2048]{1,0:T(8,128)(2,1)} %value_up_ref.5) | copy-start | bytes 6291460
  9.5 28.2 %copy-start.4 = (bf16[64,64,256]{2,1,0:T(8,128)(2,1)S(1)}, bf16[64,64,256]{2,1,0:T(8,128)(2,1)}, u32[]{:S(2)}) copy-start(bf16[64,64,256]{2,1,0:T(8,128)(2,1)} %rope_ref.1) | copy-start | bytes 6291460
  9.5 28.2 %copy-start.12 = (s32[64]{0:T(128)S(1)}, s32[64]{0:T(128)}, u32[]{:S(2)}) copy-start(s32[64]{0:T(128)} %lengths_ref.1) | copy-start | bytes 772

commit v6 on v5

--- a/solution.py
+++ b/solution.py
@@ -20,7 +20,7 @@
 DIGIT = 256
 NT = (((1,), (1,)), ((), ()))
 TN = (((0,), (0,)), ((), ()))
-VMEM_BYTES = 40 * 1024 * 1024
+VMEM_BYTES = 56 * 1024 * 1024
 
 
 def mm(a, b, dims=(((1,), (0,)), ((), ()))):

time: 76.5 us -> 76.2 us (level)
  Pallas kernels: 66.5 us -> 74.8 us
  local copies, waits for them, and re-layouts: 8.86 us -> 0.6 us
    unnamed x26 -> x0, local copies, waits for them, and re-layouts: 8.77 us -> none
    pallas_call x1, Pallas kernels: 17.8 us -> 21.1 us  [decode_attention(): pl.pallas_call(functools.partial(decode_kernel, per_step, head_count), ou...]
    pallas_call x1, Pallas kernels: 2.06 us -> 4.13 us  [join(): pl.pallas_call(join_kernel, out_shape=(jax.ShapeDtypeStruct((tokens, tota...]
    pallas_call x1, Pallas kernels: 18.4 us -> 20.2 us  [last_call(): pl.pallas_call(functools.partial(last_kernel, heads), out_shape=(jax.Shap...]
    pallas_call x1, Pallas kernels: 28.2 us -> 29.3 us  [first_call(): pl.pallas_call(functools.partial(first_kernel, heads), out_shape=(jax.Sha...]
where the time goes in v6:
time: 76.2 us; the launch traced here: 76 us
  Pallas kernels  74.8 us (98%)
    pallas_call x1, Pallas kernels, first_call(): pl.pallas_call(functools.partial(first_kernel, heads), out_shape=(jax.Sha...  29.3 us
    pallas_call x1, Pallas kernels, decode_attention(): pl.pallas_call(functools.partial(decode_kernel, per_step, head_count), ou...  21.1 us
    pallas_call x1, Pallas kernels, last_call(): pl.pallas_call(functools.partial(last_kernel, heads), out_shape=(jax.Shap...  20.2 us
    pallas_call x1, Pallas kernels, join(): pl.pallas_call(join_kernel, out_shape=(jax.ShapeDtypeStruct((tokens, tota...  4.13 us

profile of v6, /device:TPU:0, one launch (start us, length us, event | category | flops | bytes accessed | tf_op | source)
XLA Modules:
  0.0 76.0 jit_solution(6186459562218658704)
XLA Ops:
  0.7 0.6 broadcast_in_dim_tile.5.frequency_ref
  1.2 29.3 %shard_map.140 = (bf16[8,16,3200]{2,1,0:T(8,128)(2,1)}, s32[1,64]{1,0:T(1,128)}, bf16[4,128,1536]{2,1,0:T(8,128)(2,1)}, bf16[4,128,512]{2,1,0:T(8,128)(2,1)}, bf...) custom-call(s32[1,64]{1,0:T(1,128)} %bitcast.3, s32[1,64]{1,0:T(1,128)} %bitcast.4, bf16[64,3072]{1,0:T(8,128)(2,1)} %queries_ref.1, ...), custom_call_target="tpu_custom_call" | custom-call | tf_op jit(solution)/shard_map/pallas_call | solution.py:572
  30.6 21.1 %shard_map.141.answers_ref = bf16[8,16,2048]{2,1,0:T(8,128)(2,1)} custom-call(s32[64]{0:T(128)} %lengths_ref.1, bf16[8,16,3200]{2,1,0:T(8,128)(2,1)} %get-tuple-element.12.payload_ref, bf16[512,2048]{1,0:T(8,128)(2,1)} %key_up_ref.5, bf16[512,2048]{1,0:T(8,128)(2,1)} %value_up_ref.5, bf16[64,256,512]{2,1,0:T(8,128)(2,1)} %cache_ref.1, ...), custom_call_target="tpu_custom_call" | custom-call | flops 4831838208 | bytes 17596416 | tf_op jit(solution)/shard_map/pallas_call | solution.py:419
  51.7 20.2 %shard_map.142 = (bf16[64,2048]{1,0:T(8,128)(2,1)}, bf16[512,1536]{1,0:T(8,128)(2,1)}) custom-call(s32[1,64]{1,0:T(1,128)} %get-tuple-element.11.back_ref, bf16[8,16,2048]{2,1,0:T(8,128)(2,1)} %shard_map.141.answers_ref, bf16[4,128,1536]{2,1,0:T(8,128)(2,1)} %get-tuple-element.13.query_latents_ref, bf16[4,128,512]{2,1,0:T(8,128)(2,1)} %get-tuple-element.14.latents_ref, ...), custom_call_target="tpu_custom_call" | custom-call | tf_op jit(solution)/shard_map/pallas_call | solution.py:622
  71.9 4.1 %shard_map.143 = (bf16[512,2048]{1,0:T(8,128)(2,1)}, bf16[64,2048]{1,0:T(8,128)(2,1)}) custom-call(bf16[512,512]{1,0:T(8,128)(2,1)} %get-tuple-element.10.first_ref, bf16[512,1536]{1,0:T(8,128)(2,1)} %get-tuple-element.16.second_ref, bf16[64,2048]{1,0:T(8,128)(2,1)} %get-tuple-element.17.decoded_ref), custom_call_target="tpu_custom_call" | custom-call | tf_op jit(solution)/shard_map/pallas_call | solution.py:659
  (2 shorter events, 0.0 us)
